TPU v7x, 32 devices: a whole 2x2x4 slice. The times are simulated.
32 devices in a mesh: parts: 2 (over y), blk: 4 (over z), reader: 4 (over x, core), sub: 1.
Axes of the slice: x: 2, y: 2, z: 4, core: 2. Of those that a mesh axis runs over, the one named last changes fastest.
Arguments:
- images: bfloat16 [3072, 8192], P(('parts', 'blk', 'reader'), 'sub'), parts along dimension 0, may hold values from -40 to 40
- routes: int32 [3072, 2], P(('parts', 'blk', 'reader')), parts along dimension 0, may hold values from 0 to 3, all different within a row; in each aligned block of 96 rows (0 to 95, 96 to 191, ...) at most 96 rows name the same one
- projections: bfloat16 [8, 128, 8192], P(('parts', 'reader'), 'blk', 'sub'), parts along dimension 0, may hold values from -8 to 8
- noise_weights: float32 [16384], P(('parts', 'sub')), parts along dimension 0, may hold values from 0.3 to 3
Outputs:
- weighted_sums: float32 [8, 128, 8192], P(('parts', 'reader'), 'blk', 'sub'), parts along dimension 0
- normalizer: float32 [3072], P(('parts', 'blk', 'reader')), parts along dimension 0
There are 2 independent parts, one for each index of `parts`. A program takes and returns all parts, laid end to end along the dimension named above; each array names one. Nothing has to cross between parts.
Inputs may be any that keep to these rules, and one draw needn't show every extreme that they name: `routes`: each row names 2 different class groups. In the rows of one device (aligned blocks of 96 rows) no group is named by more than 96 rows, a bound that some block reaches.
All inputs are finite; a program needn't handle non-finite values.
Results may differ from a plain program's by a relative error of at most 0.019.
Values may be sent and summed in bfloat16 or wider, within the bound.
A program may use at most 64 MiB of HBM per device.

v0:
```python
from functools import partial

import jax
import jax.numpy as jnp
from jax import lax
from jax.experimental import pallas as pl
from jax.experimental.pallas import tpu as pltpu
from jax.sharding import PartitionSpec as P

MESH = pl.DeviceIdType.MESH


def from_behind(block, axis, distance):
    devices = range(lax.axis_size(axis))
    route = [((i - distance) % len(devices), i) for i in devices]
    return lax.ppermute(block, axis, route)


def slot_positions(route_block):
    flat = route_block.reshape(-1)
    order = jnp.arange(flat.shape[0], dtype=jnp.int32)
    earlier = (order[None, :] < order[:, None]) & (flat[None, :] == flat[:, None])
    return jnp.sum(earlier.astype(jnp.int32), axis=1).reshape(route_block.shape)


def combine_stats(row_peaks, row_totals):
    highest = jnp.max(row_peaks, axis=-1)
    spread = row_totals * jnp.exp(row_peaks - highest[..., None])
    return highest + jnp.log(jnp.sum(spread, axis=-1))


def routed(images, routes, projections, noise_weights):
    groups = lax.axis_size("reader")
    cycle_size = lax.axis_size("blk")
    my_group = lax.axis_index("reader")
    my_member = lax.axis_index("blk")
    per_device, top_count = routes.shape
    half_width = images.shape[1]
    capacity = min(per_device, 2 * per_device * top_count // groups)
    slot_count = groups * capacity
    ref_count = projections.shape[1]
    all_refs = ref_count * cycle_size
    anchor = jnp.zeros((), jnp.int32)
    own_index = slot_positions(routes)
    own_target = routes * capacity + own_index
    sources = jnp.broadcast_to(jnp.arange(per_device, dtype=jnp.int32)[:, None], routes.shape)
    picker = (
        jnp.full((slot_count,), per_device, jnp.int32)
        .at[own_target.reshape(-1)]
        .set(sources.reshape(-1))
    )
    padded = jnp.concatenate([images, jnp.zeros((1, half_width), images.dtype)], axis=0)
    outgoing = padded[picker].reshape(groups, capacity, half_width)
    received = lax.all_to_all(outgoing, "reader", split_axis=0, concat_axis=0, tiled=True).reshape(
        slot_count, half_width
    )
    every_route = lax.all_gather(routes, "reader", axis=0, tiled=True).reshape(
        groups, per_device, top_count
    )
    every_index = jax.vmap(slot_positions)(every_route)
    senders = jnp.arange(groups, dtype=jnp.int32)[:, None, None]
    landing = jnp.where(every_route == my_group, senders * capacity + every_index, slot_count)
    live_slot = jnp.zeros((slot_count,), jnp.int32).at[landing.reshape(-1)].set(1, mode="drop") > 0

    def score_block(ref_block):
        scaled = ref_block.astype(jnp.float32) * noise_weights[None, :]
        weighted = scaled.astype(jnp.bfloat16)
        penalty = 0.5 * jnp.sum(scaled * ref_block.astype(jnp.float32), axis=1)
        partial_scores = lax.dot_general(
            weighted, received, (((1,), (1,)), ((), ())), preferred_element_type=jnp.float32
        )
        return partial_scores - penalty[:, None]

    def cycle_turn(rotation, carry):
        ref_block, score_table = carry
        position = (my_member - rotation) % cycle_size
        score_table = lax.dynamic_update_slice(
            score_table, score_block(ref_block)[None], (position, anchor, anchor)
        )
        ref_block = from_behind(ref_block, "blk", 1)
        return (ref_block, score_table)

    empty_table = jnp.zeros((cycle_size, ref_count, slot_count), jnp.float32)
    ref_block, score_table = lax.fori_loop(
        0, cycle_size - 1, cycle_turn, (projections[0], empty_table)
    )
    position = (my_member + 1) % cycle_size
    score_table = lax.dynamic_update_slice(
        score_table, score_block(ref_block)[None], (position, anchor, anchor)
    )
    score_table = lax.psum(score_table, "sub")
    scores = score_table.reshape(all_refs, slot_count)
    row_peak = jnp.max(scores, axis=0)
    row_total = jnp.sum(jnp.exp(scores - row_peak[None, :]), axis=0)
    back_peak, back_total = (
        lax.all_to_all(
            row_peak.reshape(groups, capacity), "reader", split_axis=0, concat_axis=0, tiled=True
        ),
        lax.all_to_all(
            row_total.reshape(groups, capacity), "reader", split_axis=0, concat_axis=0, tiled=True
        ),
    )
    normalizer = combine_stats(
        back_peak.reshape(-1)[own_target], back_total.reshape(-1)[own_target]
    )
    outgoing_norm = (
        jnp.zeros((slot_count,), jnp.float32)
        .at[own_target.reshape(-1)]
        .set(jnp.repeat(normalizer, top_count))
    )
    slot_norm = lax.all_to_all(
        outgoing_norm.reshape(groups, capacity), "reader", split_axis=0, concat_axis=0, tiled=True
    ).reshape(slot_count)
    exponent = jnp.where(live_slot[None, :], scores - slot_norm[None, :], -jnp.inf)
    posterior = jnp.exp(exponent).astype(jnp.bfloat16)
    summed = lax.psum_scatter(
        jnp.dot(posterior, received, preferred_element_type=jnp.float32).astype(jnp.bfloat16),
        "blk",
        scatter_dimension=0,
        tiled=True,
    ).astype(jnp.float32)
    return (summed[None], normalizer)


def flipped(number, mask, size):
    result, bit = 0, 1
    while bit < size:
        digit = lax.rem(lax.div(number, bit), 2)
        result = result + bit * ((1 - digit) if mask & bit else digit)
        bit *= 2
    return result


def kernel(
    R, B,
    images, routes_in, proj, noise_in,
    out, norm,
    routes, noise,
    X, PR, S, SR, Q, PART, UR, DR, US, DS, O,
    loc, p_snd, p_rcv, x_snd, x_rcv, gu_snd, gd_snd, s_snd, s_rcv, q_snd, q_rcv,
    u_snd, u_rcv, d_snd, d_rcv, o_snd, o_rcv,
):
    r = lax.axis_index("reader")
    b = lax.axis_index("blk")
    rows = images.shape[0]
    refs = proj.shape[0]
    Cs = X.shape[2]
    T, tile = O.shape[0], O.shape[3]
    width = R * refs
    far = [k for k in range(R - 1, 1, -1)]
    masks = far + [1]
    order = [1] + far[::-1]
    peers = {k: flipped(r, k, R) for k in masks}
    not_top = b < B - 1
    not_bottom = b > 0

    def span(i):
        return pl.ds(pl.multiple_of(i * Cs, Cs), Cs)

    def to_reader(src, dst, snd, rcv, k):
        return pltpu.make_async_remote_copy(
            src_ref=src, dst_ref=dst, send_sem=snd, recv_sem=rcv,
            device_id={"reader": peers[k]}, device_id_type=MESH,
        )

    def to_blk(src, dst, snd, rcv, step):
        return pltpu.make_async_remote_copy(
            src_ref=src, dst_ref=dst, send_sem=snd, recv_sem=rcv,
            device_id={"blk": b + step}, device_id_type=MESH,
        )

    def proj_copy(k):
        return to_reader(proj.at[:, span(peers[k])], PR.at[b, r], p_snd.at[k], p_rcv.at[b, r], k)

    def image_copy(k):
        return to_reader(images.at[:, span(peers[k])], X.at[r], x_snd.at[k], x_rcv.at[r], k)

    def gather_copy(src, g, step):
        snd = gu_snd if step > 0 else gd_snd
        return to_blk(PR.at[src, g], PR.at[src, g], snd.at[src, g], p_rcv.at[src, g], step)

    def score_copy(src, k):
        return to_reader(S.at[src, peers[k]], SR.at[src, r], s_snd.at[src, k], s_rcv.at[src, r], k)

    def post_copy(c, k):
        return to_reader(Q.at[c, r], Q.at[c, r], q_snd.at[c, k], q_rcv.at[c, r], k)

    def up_copy(d, t):
        return to_blk(US.at[d, t], UR.at[d, t], u_snd.at[d, t], u_rcv.at[d, t], 1)

    def down_copy(d, t):
        return to_blk(DS.at[d, t], DR.at[d, t], d_snd.at[d, t], d_rcv.at[d, t], -1)

    def out_span(i, t):
        return out.at[:, pl.ds(pl.multiple_of(i * Cs + t * tile, tile), tile)]

    def out_copy(t, k):
        return to_reader(O.at[t, peers[k]], out_span(r, t), o_snd.at[t, k], o_rcv.at[t, r], k)

    def own_out(t):
        return pltpu.make_async_copy(O.at[t, r], out_span(r, t), o_snd.at[t, 0])

    def arrived(dst, sem):
        to_reader(dst, dst, sem, sem, 1).wait_recv()

    own_proj = pltpu.make_async_copy(proj.at[:, span(r)], PR.at[b, r], loc.at[0])
    own_image = pltpu.make_async_copy(images.at[:, span(r)], X.at[r], loc.at[1])
    own_proj.start()
    noise_copy = pltpu.make_async_copy(noise_in, noise, loc.at[2])
    noise_copy.start()
    routes_copy = pltpu.make_async_copy(routes_in, routes, loc.at[3])
    routes_copy.start()

    barrier = pltpu.get_barrier_semaphore()
    for k in masks:
        pl.semaphore_signal(barrier, inc=1, device_id={"reader": peers[k]}, device_id_type=MESH)

    @pl.when(not_top)
    def _():
        pl.semaphore_signal(barrier, inc=1, device_id={"blk": b + 1}, device_id_type=MESH)

    @pl.when(not_bottom)
    def _():
        pl.semaphore_signal(barrier, inc=1, device_id={"blk": b - 1}, device_id_type=MESH)

    pl.semaphore_wait(
        barrier, (R - 1) + not_top.astype(jnp.int32) + not_bottom.astype(jnp.int32)
    )

    for k in order:
        proj_copy(k).start()
    own_proj.wait()

    def send_own(g):
        @pl.when(not_top)
        def _():
            gather_copy(b, g, 1).start()

        @pl.when(not_bottom)
        def _():
            gather_copy(b, g, -1).start()

    send_own(r)
    own_image.start()
    for k in order:
        arrived(PR.at[b, peers[k]], p_rcv.at[b, peers[k]])
        send_own(peers[k])
    for k in masks:
        image_copy(k).start()

    def score_chunk(src):
        scores = jnp.zeros((R * rows, width), jnp.float32)
        penalty = jnp.zeros((width, 128), jnp.float32)
        for t in range(Cs // tile):
            cut = pl.ds(t * tile, tile)
            refs_f = PR[src, :, :, cut].reshape(width, tile).astype(jnp.float32)
            weights = noise[pl.ds(pl.multiple_of(r * Cs + t * tile, tile), tile)]
            scaled = refs_f * weights[None, :]
            scores = scores + lax.dot_general(
                X[:, :, cut].reshape(R * rows, tile), scaled.astype(jnp.bfloat16),
                (((1,), (1,)), ((), ())), preferred_element_type=jnp.float32,
            )
            squares = scaled * refs_f
            for lane in range(0, tile, 128):
                penalty = penalty + squares[:, lane : lane + 128]
        penalty_row = lax.dot_general(
            jnp.full((8, 128), 0.5, jnp.float32), penalty,
            (((1,), (1,)), ((), ())), preferred_element_type=jnp.float32,
            precision=lax.Precision.HIGHEST,
        )
        scores = scores - penalty_row[0:1]
        S[src] = scores.reshape(R, rows, width)
        for k in masks:
            score_copy(src, k).start()

    gather_order = [0] + order

    def forward(dist, carry):
        below, above = b - dist, b + dist
        for k in gather_order:
            g = flipped(r, k, R)

            @pl.when(below >= 0)
            def _():
                arrived(PR.at[below, g], p_rcv.at[below, g])

                @pl.when(not_top)
                def _():
                    gather_copy(below, g, 1).start()

            @pl.when(above < B)
            def _():
                arrived(PR.at[above, g], p_rcv.at[above, g])

                @pl.when(not_bottom)
                def _():
                    gather_copy(above, g, -1).start()

        return carry

    def score_pair(dist, carry):
        @pl.when(b - dist >= 0)
        def _():
            score_chunk(b - dist)

        @pl.when(b + dist < B)
        def _():
            score_chunk(b + dist)

        return carry

    lax.fori_loop(1, B - 1, forward, 0)
    noise_copy.wait()
    routes_copy.wait()
    own_image.wait()
    for k in order:
        arrived(X.at[peers[k]], x_rcv.at[peers[k]])
    score_chunk(b)
    lax.fori_loop(1, B - 1, score_pair, 0)
    forward(B - 1, 0)
    score_pair(B - 1, 0)

    lane_group = lax.broadcasted_iota(jnp.int32, (rows, width), 1) // refs
    diagonal = lax.broadcasted_iota(jnp.int32, (rows, rows), 0) == lax.broadcasted_iota(
        jnp.int32, (rows, rows), 1
    )

    def column(row):
        return jnp.sum(jnp.where(diagonal, row, 0.0), axis=1, keepdims=True).astype(jnp.int32)

    names = routes[...].astype(jnp.float32)
    named = (column(names[0:1]) == lane_group) | (column(names[1:2]) == lane_group)
    chunks = []
    for c in range(B):
        total = S[c, r]
        for k in masks:
            arrived(SR.at[c, peers[k]], s_rcv.at[c, peers[k]])
            total = total + SR[c, peers[k]]
        chunks.append(jnp.where(named, total, -jnp.inf))
    highest = chunks[0]
    for c in range(1, B):
        highest = jnp.maximum(highest, chunks[c])
    highest = jnp.max(highest, axis=1, keepdims=True)
    spread = jnp.exp(chunks[0] - highest)
    for c in range(1, B):
        spread = spread + jnp.exp(chunks[c] - highest)
    normalizer = highest + jnp.log(jnp.sum(spread, axis=1, keepdims=True))
    for c in range(B):
        Q[c, r] = jnp.exp(chunks[c] - normalizer).astype(jnp.bfloat16)
    lower = (2 * b < B).astype(jnp.int32)
    for i in range(B):
        for k in masks:
            post_copy(i + lower * (B - 1 - 2 * i), k).start()
    norm[...] = jnp.broadcast_to(normalizer, norm.shape)
    def product(d, t):
        cut = pl.ds(pl.multiple_of(t * tile, tile), tile)
        return lax.dot_general(
            Q[d].reshape(R * rows, width), X[:, :, cut].reshape(R * rows, tile),
            (((0,), (0,)), ((), ())), preferred_element_type=jnp.float32,
        )

    def whole(d):
        for k in order:
            arrived(Q.at[d, peers[k]], q_rcv.at[d, peers[k]])

    pieces = (B - 1) * T

    def reduce_step(turn, carry):
        n = turn - b
        up, t = B - 1 - n // T, n % T

        @pl.when((n >= 0) & (n < pieces) & (up > b))
        def _():
            @pl.when(t == 0)
            def _():
                whole(up)

            own = product(up, t)

            @pl.when(b == 0)
            def _():
                US[up, t] = own.astype(jnp.bfloat16)

            @pl.when(b > 0)
            def _():
                arrived(UR.at[up, t], u_rcv.at[up, t])
                US[up, t] = (own + UR[up, t].astype(jnp.float32)).astype(jnp.bfloat16)

            up_copy(up, t).start()

        m = turn - (B - 1 - b)
        down, s = m // T, m % T

        @pl.when((m >= 0) & (m < pieces) & (down < b))
        def _():
            @pl.when(s == 0)
            def _():
                whole(down)

            own = product(down, s)

            @pl.when(b == B - 1)
            def _():
                DS[down, s] = own.astype(jnp.bfloat16)

            @pl.when(b < B - 1)
            def _():
                arrived(DR.at[down, s], d_rcv.at[down, s])
                DS[down, s] = (own + DR[down, s].astype(jnp.float32)).astype(jnp.bfloat16)

            down_copy(down, s).start()

        return carry

    lax.fori_loop(0, pieces + B - 1, reduce_step, 0)

    whole(b)
    for t in range(T):
        PART[t] = product(b, t)
    for t in range(T):
        @pl.when(not_bottom)
        def _():
            arrived(UR.at[b, t], u_rcv.at[b, t])
            PART[t] = PART[t] + UR[b, t].astype(jnp.float32)

        @pl.when(not_top)
        def _():
            arrived(DR.at[b, t], d_rcv.at[b, t])
            PART[t] = PART[t] + DR[b, t].astype(jnp.float32)

        O[t] = PART[t].reshape(R, refs, tile).astype(jnp.bfloat16)
        for k in masks:
            out_copy(t, k).start()
        own_out(t).start()

    for k in masks:
        proj_copy(k).wait_send()
        image_copy(k).wait_send()

    def sent(i, carry):
        for k in masks:
            score_copy(i, k).wait_send()
            post_copy(i, k).wait_send()
        for g in range(R):
            @pl.when(not_top & (i <= b))
            def _():
                gather_copy(i, g, 1).wait_send()

            @pl.when(not_bottom & (i >= b))
            def _():
                gather_copy(i, g, -1).wait_send()

        for t in range(T):
            @pl.when(i > b)
            def _():
                up_copy(i, t).wait_send()

            @pl.when(i < b)
            def _():
                down_copy(i, t).wait_send()

        return carry

    lax.fori_loop(0, B, sent, 0)
    for t in range(T):
        own_out(t).wait()
        for k in masks:
            out_copy(t, k).wait_send()
            arrived(out_span(peers[k], t), o_rcv.at[t, peers[k]])


def split_coefficients(images, routes, projections, noise_weights):
    R, B = lax.axis_size("reader"), lax.axis_size("blk")
    rows, coef = images.shape
    refs = projections.shape[1]
    Cs, width = coef // R, R * refs
    tile = min(Cs, 512)
    T = Cs // tile
    dma = pltpu.SemaphoreType.DMA
    bf16, f32 = jnp.bfloat16, jnp.float32
    sums, norm = pl.pallas_call(
        partial(kernel, R, B),
        out_shape=(
            jax.ShapeDtypeStruct((refs, coef), bf16),
            jax.ShapeDtypeStruct((rows, 128), f32),
        ),
        in_specs=[
            pl.BlockSpec(memory_space=pltpu.HBM),
            pl.BlockSpec(memory_space=pltpu.HBM),
            pl.BlockSpec(memory_space=pltpu.HBM),
            pl.BlockSpec(memory_space=pltpu.HBM),
        ],
        out_specs=(
            pl.BlockSpec(memory_space=pl.ANY),
            pl.BlockSpec(memory_space=pltpu.VMEM),
        ),
        scratch_shapes=[
            pltpu.VMEM((2, rows), jnp.int32),
            pltpu.VMEM((coef,), f32),
            pltpu.VMEM((R, rows, Cs), bf16),
            pltpu.VMEM((B, R, refs, Cs), bf16),
            pltpu.VMEM((B, R, rows, width), f32),
            pltpu.VMEM((B, R, rows, width), f32),
            pltpu.VMEM((B, R, rows, width), bf16),
            pltpu.VMEM((T, width, tile), f32),
            pltpu.VMEM((B, T, width, tile), bf16),
            pltpu.VMEM((B, T, width, tile), bf16),
            pltpu.VMEM((B, T, width, tile), bf16),
            pltpu.VMEM((B, T, width, tile), bf16),
            pltpu.VMEM((T, R, refs, tile), bf16),
            dma((4,)),
            dma((R,)), dma((B, R)), dma((R,)), dma((R,)),
            dma((B, R)), dma((B, R)),
            dma((B, R)), dma((B, R)),
            dma((B, R)), dma((B, R)),
            dma((B, T)), dma((B, T)), dma((B, T)), dma((B, T)),
            dma((T, R)), dma((T, R)),
        ],
        compiler_params=pltpu.CompilerParams(
            collective_id=0, has_side_effects=True, vmem_limit_bytes=64 * 1024 * 1024 - 65536
        ),
        cost_estimate=pl.CostEstimate(
            flops=4 * R * rows * B * width * Cs, bytes_accessed=4 * rows * coef, transcendentals=0
        ),
    )(images, routes.T, projections[0], noise_weights)
    return (sums.astype(f32)[None], norm[:, 0])


def solution(mesh):
    sizes = dict(mesh.shape)
    readers = sizes["reader"]
    direct = sizes["sub"] == 1 and readers > 1 and readers & (readers - 1) == 0
    return jax.shard_map(
        split_coefficients if direct else routed,
        mesh=mesh,
        in_specs=(
            P(("parts", "blk", "reader"), "sub"),
            P(("parts", "blk", "reader"), None),
            P(("parts", "reader"), "blk", "sub"),
            P(("parts", "sub")),
        ),
        out_specs=(P(("parts", "reader"), "blk", "sub"), P(("parts", "blk", "reader"))),
        check_vma=False,
    )
```

profile of v0, /device:TPU:16, one launch (start us, length us, event | category | flops | bytes accessed | tf_op | source)
XLA Modules:
  0.0 91.1 jit_solution(15215559879814534355)
XLA Ops:
  0.6 86.9 %shard_map.59 = (bf16[32,8192]{1,0:T(8,128)(2,1)}, f32[96,128]{1,0:T(8,128)}) custom-call(bf16[96,8192]{1,0:T(8,128)(2,1)} %images.1, s32[2,96]{1,0:T(2,128)} %bitcast.6, bf16[32,8192]{1,0:T(8,128)(2,1)} %bitcast.5, f32[8192]{0:T(1024)} %noise_in.1), custom_call_target="tpu_custom_call" | custom-call | flops 1610612736 | bytes 3145728 | tf_op jit(solution)/shard_map/pallas_call | solution.py:481
  87.6 1.4 %slice_reduce_fusion = f32[96]{0:T(128)} fusion(f32[96,128]{1,0:T(8,128)} %get-tuple-element.5), kind=kLoop, calls=%fused_computation.1 | loop fusion | bytes 768 | tf_op jit(solution)/shard_map/slice | solution.py:526
  89.0 2.1 %bitcast_convert_fusion = f32[1,32,8192]{2,1,0:T(8,128)} fusion(bf16[32,8192]{1,0:T(8,128)(2,1)} %get-tuple-element.4), kind=kLoop, calls=%fused_computation | loop fusion | flops 262144 | bytes 1572864 | tf_op jit(solution)/shard_map/broadcast_in_dim | solution.py:526
where the time goes:
time: 91.3 us; the launch traced here: 91.1 us
  Pallas kernels  86.9 us (95%)
  other arithmetic  2.08 us (2%)
  local copies, waits for them, and re-layouts  1.43 us (2%)
    pallas_call x1, Pallas kernels, split_coefficients(): pl.pallas_call(partial(kernel, R, B), out_shape=(jax.ShapeDtypeStruct((re...  86.9 us
    broadcast_in_dim x1, other arithmetic, split_coefficients(): return (sums.astype(f32)[None], norm[:, 0])  2.08 us

commit v1 on v0

v1 whole, which is shorter than its diff:
```python
from functools import partial

import jax
import jax.numpy as jnp
from jax import lax
from jax.experimental import pallas as pl
from jax.experimental.pallas import tpu as pltpu
from jax.sharding import PartitionSpec as P

MESH = pl.DeviceIdType.MESH


def from_behind(block, axis, distance):
    devices = range(lax.axis_size(axis))
    route = [((i - distance) % len(devices), i) for i in devices]
    return lax.ppermute(block, axis, route)


def slot_positions(route_block):
    flat = route_block.reshape(-1)
    order = jnp.arange(flat.shape[0], dtype=jnp.int32)
    earlier = (order[None, :] < order[:, None]) & (flat[None, :] == flat[:, None])
    return jnp.sum(earlier.astype(jnp.int32), axis=1).reshape(route_block.shape)


def combine_stats(row_peaks, row_totals):
    highest = jnp.max(row_peaks, axis=-1)
    spread = row_totals * jnp.exp(row_peaks - highest[..., None])
    return highest + jnp.log(jnp.sum(spread, axis=-1))


def routed(images, routes, projections, noise_weights):
    groups = lax.axis_size("reader")
    cycle_size = lax.axis_size("blk")
    my_group = lax.axis_index("reader")
    my_member = lax.axis_index("blk")
    per_device, top_count = routes.shape
    half_width = images.shape[1]
    capacity = min(per_device, 2 * per_device * top_count // groups)
    slot_count = groups * capacity
    ref_count = projections.shape[1]
    all_refs = ref_count * cycle_size
    anchor = jnp.zeros((), jnp.int32)
    own_index = slot_positions(routes)
    own_target = routes * capacity + own_index
    sources = jnp.broadcast_to(jnp.arange(per_device, dtype=jnp.int32)[:, None], routes.shape)
    picker = (
        jnp.full((slot_count,), per_device, jnp.int32)
        .at[own_target.reshape(-1)]
        .set(sources.reshape(-1))
    )
    padded = jnp.concatenate([images, jnp.zeros((1, half_width), images.dtype)], axis=0)
    outgoing = padded[picker].reshape(groups, capacity, half_width)
    received = lax.all_to_all(outgoing, "reader", split_axis=0, concat_axis=0, tiled=True).reshape(
        slot_count, half_width
    )
    every_route = lax.all_gather(routes, "reader", axis=0, tiled=True).reshape(
        groups, per_device, top_count
    )
    every_index = jax.vmap(slot_positions)(every_route)
    senders = jnp.arange(groups, dtype=jnp.int32)[:, None, None]
    landing = jnp.where(every_route == my_group, senders * capacity + every_index, slot_count)
    live_slot = jnp.zeros((slot_count,), jnp.int32).at[landing.reshape(-1)].set(1, mode="drop") > 0

    def score_block(ref_block):
        scaled = ref_block.astype(jnp.float32) * noise_weights[None, :]
        weighted = scaled.astype(jnp.bfloat16)
        penalty = 0.5 * jnp.sum(scaled * ref_block.astype(jnp.float32), axis=1)
        partial_scores = lax.dot_general(
            weighted, received, (((1,), (1,)), ((), ())), preferred_element_type=jnp.float32
        )
        return partial_scores - penalty[:, None]

    def cycle_turn(rotation, carry):
        ref_block, score_table = carry
        position = (my_member - rotation) % cycle_size
        score_table = lax.dynamic_update_slice(
            score_table, score_block(ref_block)[None], (position, anchor, anchor)
        )
        ref_block = from_behind(ref_block, "blk", 1)
        return (ref_block, score_table)

    empty_table = jnp.zeros((cycle_size, ref_count, slot_count), jnp.float32)
    ref_block, score_table = lax.fori_loop(
        0, cycle_size - 1, cycle_turn, (projections[0], empty_table)
    )
    position = (my_member + 1) % cycle_size
    score_table = lax.dynamic_update_slice(
        score_table, score_block(ref_block)[None], (position, anchor, anchor)
    )
    score_table = lax.psum(score_table, "sub")
    scores = score_table.reshape(all_refs, slot_count)
    row_peak = jnp.max(scores, axis=0)
    row_total = jnp.sum(jnp.exp(scores - row_peak[None, :]), axis=0)
    back_peak, back_total = (
        lax.all_to_all(
            row_peak.reshape(groups, capacity), "reader", split_axis=0, concat_axis=0, tiled=True
        ),
        lax.all_to_all(
            row_total.reshape(groups, capacity), "reader", split_axis=0, concat_axis=0, tiled=True
        ),
    )
    normalizer = combine_stats(
        back_peak.reshape(-1)[own_target], back_total.reshape(-1)[own_target]
    )
    outgoing_norm = (
        jnp.zeros((slot_count,), jnp.float32)
        .at[own_target.reshape(-1)]
        .set(jnp.repeat(normalizer, top_count))
    )
    slot_norm = lax.all_to_all(
        outgoing_norm.reshape(groups, capacity), "reader", split_axis=0, concat_axis=0, tiled=True
    ).reshape(slot_count)
    exponent = jnp.where(live_slot[None, :], scores - slot_norm[None, :], -jnp.inf)
    posterior = jnp.exp(exponent).astype(jnp.bfloat16)
    summed = lax.psum_scatter(
        jnp.dot(posterior, received, preferred_element_type=jnp.float32).astype(jnp.bfloat16),
        "blk",
        scatter_dimension=0,
        tiled=True,
    ).astype(jnp.float32)
    return (summed[None], normalizer)


def paired(
    images, routes_in, proj, noise_in,
    out, norm,
    routes, noise, X, XF, PR, S, SR, QP, QO, QF, QT, QTF, PROD, TE, RE, TM, RM, TI, RI, O,
    loc, px_snd, pb_snd, pm_snd, pc_snd, p_rcv, xx_snd, xc_snd, x_rcv, xf_snd, xfc_snd, xf_rcv,
    s_snd, s_rcv, q_snd, q_rcv, qf_snd, qf_rcv, e_snd, e_rcv, m_snd, m_rcv, i_snd, i_rcv,
    own_snd, o_snd, o_rcv,
):
    r = lax.axis_index("reader")
    b = lax.axis_index("blk")
    x, c = r // 2, r % 2
    rx, rc = (r + 2) % 4, x * 2 + 1 - c
    rd = (rc + 2) % 4
    side = b // 2
    inner, end = 1 + side, 3 * side
    far_inner, far_end = 2 - side, 3 - 3 * side
    buddy, across = inner + end - b, 3 - b
    is_end = b == end
    is_inner = b == inner
    rows = images.shape[0]
    refs = proj.shape[0]
    H = X.shape[4 - 1]
    F = H // 2
    T, tile = O.shape[0], O.shape[3]
    TF = F // tile
    width = 4 * refs
    halves = (0, 1)

    def remote(src, dst, snd, rcv, **where):
        return pltpu.make_async_remote_copy(
            src_ref=src, dst_ref=dst, send_sem=snd, recv_sem=rcv,
            device_id=where, device_id_type=MESH,
        )

    def arrived(dst, sem):
        remote(dst, dst, sem, sem, reader=rx).wait_recv()

    def columns(i, h):
        return pl.ds(pl.multiple_of(i * H + h * F, F), F)

    def part(src, g, h):
        return PR.at[src, g, :, pl.ds(h * F, F)]

    def own_piece(h):
        return proj.at[:, columns(x, h)]

    def proj_x(h):
        return remote(proj.at[:, columns(1 - x, h)], part(b, r, h), px_snd.at[h], p_rcv.at[b, r, h], reader=rx)

    def to_core(piece, src, g, h):
        return remote(piece, part(src, g, h), pc_snd.at[src, g, h], p_rcv.at[src, g, h], reader=rc)

    def to_buddy(piece, src, g, h):
        return remote(piece, part(src, g, h), pb_snd.at[src, g, h], p_rcv.at[src, g, h], blk=buddy)

    def to_across(piece, src, g, h):
        return remote(piece, part(src, g, h), pm_snd.at[src, g, h], p_rcv.at[src, g, h], blk=across)

    def image_x(h):
        return remote(
            images.at[:, columns(1 - x, h)], X.at[c, x, :, pl.ds(h * F, F)],
            xx_snd.at[h], x_rcv.at[c, x, h], reader=rx,
        )

    def own_image_core():
        return remote(
            images.at[:, pl.ds(pl.multiple_of(x * H, H), H)], X.at[c, x],
            xc_snd.at[0], x_rcv.at[c, x, 0], reader=rc,
        )

    def other_image_core():
        return remote(X.at[c, 1 - x], X.at[c, 1 - x], xc_snd.at[1], x_rcv.at[c, 1 - x, 0], reader=rc)

    def own_far():
        return remote(images.at[:, columns(x, 0)], XF.at[c, x], xf_snd.at[0], xf_rcv.at[c, x], blk=buddy)

    def other_far():
        return remote(
            X.at[c, 1 - x, :, pl.ds(0, F)], XF.at[c, 1 - x], xf_snd.at[1], xf_rcv.at[c, 1 - x], blk=buddy
        )

    def far_core(i):
        return remote(XF.at[c, i], XF.at[c, i], xfc_snd.at[i], xf_rcv.at[c, i], reader=rc)

    def score_copy(src):
        return remote(S.at[src, 1 - x], SR.at[src], s_snd.at[src], s_rcv.at[src], reader=rx)

    def post_copy(k):
        source, to = ((QP.at[:, c, x], rx), (QO, rc), (QO, rd))[k]
        return remote(source, QP.at[:, c, x], q_snd.at[k], q_rcv.at[c, x], reader=to)

    def post_far(i, j):
        return remote(QP.at[:, i, j], QF.at[:, i, j], qf_snd.at[i, j], qf_rcv.at[i, j], blk=buddy)

    def end_copy(k, t):
        return remote(TE.at[k, t], RE.at[k, t], e_snd.at[k, t], e_rcv.at[k, t], blk=buddy)

    def middle_copy(k, t):
        return remote(TM.at[k, t], RM.at[k, t], m_snd.at[k, t], m_rcv.at[k, t], blk=across)

    def inner_copy(t):
        return remote(TI.at[t], RI.at[t], i_snd.at[t], i_rcv.at[t], blk=buddy)

    def out_span(i, t):
        return out.at[:, pl.ds(pl.multiple_of(i * H + t * tile, tile), tile)]

    def out_x(src, t):
        return remote(src.at[t, 1 - x], out_span(x, t), o_snd.at[t], o_rcv.at[t], reader=rx)

    def out_own(src, t):
        return pltpu.make_async_copy(src.at[t, x], out_span(x, t), own_snd.at[t])

    own_proj = pltpu.make_async_copy(proj.at[:, pl.ds(pl.multiple_of(x * H, H), H)], PR.at[b, r], loc.at[0])
    own_image = pltpu.make_async_copy(
        images.at[:, pl.ds(pl.multiple_of(x * H, H), H)], X.at[c, x], loc.at[1]
    )
    noise_copy = pltpu.make_async_copy(
        noise_in.at[pl.ds(pl.multiple_of(x * H, H), H)], noise, loc.at[2]
    )
    routes_copy = pltpu.make_async_copy(routes_in, routes, loc.at[3])

    barrier = pltpu.get_barrier_semaphore()
    for k in (rx, rc, rd):
        pl.semaphore_signal(barrier, inc=1, device_id={"reader": k}, device_id_type=MESH)
    pl.semaphore_signal(barrier, inc=1, device_id={"blk": buddy}, device_id_type=MESH)

    @pl.when(is_inner)
    def _():
        pl.semaphore_signal(barrier, inc=1, device_id={"blk": across}, device_id_type=MESH)

    own_proj.start()
    own_image.start()
    noise_copy.start()
    routes_copy.start()
    pl.semaphore_wait(barrier, 4 + is_inner.astype(jnp.int32))

    for h in halves:
        proj_x(h).start()
        to_buddy(own_piece(h), b, r, h).start()

        @pl.when(is_inner)
        def _():
            to_across(own_piece(h), b, r, h).start()

    for h in halves:
        to_core(own_piece(h), b, r, h).start()
    own_image_core().start()
    for h in halves:
        piece = part(b, rx, h)
        arrived(piece, p_rcv.at[b, rx, h])
        to_buddy(piece, b, rx, h).start()

        @pl.when(is_inner)
        def _():
            to_across(piece, b, rx, h).start()

        image_x(h).start()
        to_core(piece, b, rx, h).start()

    pieces = ((r, 0), (r, 1), (rx, 0), (rx, 1))

    @pl.when(is_end)
    def _():
        own_far().start()
        for g, h in pieces:
            arrived(part(buddy, g, h), p_rcv.at[buddy, g, h])
            to_core(part(buddy, g, h), buddy, g, h).start()
        arrived(X.at[c, 1 - x, :, pl.ds(0, F)], x_rcv.at[c, 1 - x, 0])
        other_far().start()
        for g, h in pieces:
            arrived(part(far_inner, g, h), p_rcv.at[far_inner, g, h])
            to_core(part(far_inner, g, h), far_inner, g, h).start()
        arrived(X.at[c, 1 - x, :, pl.ds(F, F)], x_rcv.at[c, 1 - x, 1])

    @pl.when(is_inner)
    def _():
        for g, h in pieces:
            piece = part(buddy, g, h)
            arrived(piece, p_rcv.at[buddy, g, h])
            to_across(piece, buddy, g, h).start()
            to_core(piece, buddy, g, h).start()
            piece = part(far_inner, g, h)
            arrived(piece, p_rcv.at[far_inner, g, h])
            to_buddy(piece, far_inner, g, h).start()
            to_core(piece, far_inner, g, h).start()
        for g, h in pieces:
            piece = part(far_end, g, h)
            arrived(piece, p_rcv.at[far_end, g, h])
            to_buddy(piece, far_end, g, h).start()
            to_core(piece, far_end, g, h).start()
        for h in halves:
            arrived(X.at[c, 1 - x, :, pl.ds(h * F, F)], x_rcv.at[c, 1 - x, h])

    other_image_core().start()
    own_proj.wait()
    own_image.wait()
    noise_copy.wait()
    routes_copy.wait()

    def score_half(src, h):
        scores = jnp.zeros((2 * rows, width), jnp.float32)
        penalty = jnp.zeros((width, 128), jnp.float32)
        for t in range(TF):
            cut = pl.ds(h * F + t * tile, tile)
            refs_f = PR[src, :, :, cut].reshape(width, tile).astype(jnp.float32)
            scaled = refs_f * noise[cut][None, :]
            scores = scores + lax.dot_general(
                X[c, :, :, cut].reshape(2 * rows, tile), scaled.astype(jnp.bfloat16),
                (((1,), (1,)), ((), ())), preferred_element_type=jnp.float32,
            )
            squares = scaled * refs_f
            for lane in range(0, tile, 128):
                penalty = penalty + squares[:, lane : lane + 128]
        penalty_row = lax.dot_general(
            jnp.full((8, 128), 0.5, jnp.float32), penalty,
            (((1,), (1,)), ((), ())), preferred_element_type=jnp.float32,
            precision=lax.Precision.HIGHEST,
        )
        scores = (scores - penalty_row[0:1]).reshape(2, rows, width)
        S[src] = scores if h == 0 else S[src] + scores

    def from_core(src, h):
        for g in (rc, rd):
            arrived(part(src, g, h), p_rcv.at[src, g, h])

    def score_source(i, carry):
        src = jnp.where(i == 0, b, jnp.where(i == 1, buddy, far_inner))
        for h in halves:
            from_core(src, h)
            score_half(src, h)
        score_copy(src).start()
        return carry

    lax.fori_loop(0, 3, score_source, 0)
    for h in halves:
        @pl.when(is_end)
        def _():
            for g, k in (pieces[:3], pieces[3:])[h]:
                piece = part(far_end, g, k)
                arrived(piece, p_rcv.at[far_end, g, k])
                to_core(piece, far_end, g, k).start()

        from_core(far_end, h)
        score_half(far_end, h)
    score_copy(far_end).start()

    lane = lax.broadcasted_iota(jnp.int32, (rows, width), 1)
    lane_group = lane // refs
    diagonal = lax.broadcasted_iota(jnp.int32, (rows, rows), 0) == lax.broadcasted_iota(
        jnp.int32, (rows, rows), 1
    )

    def column(row):
        return jnp.sum(jnp.where(diagonal, row, 0.0), axis=1, keepdims=True).astype(jnp.int32)

    names = routes[...].astype(jnp.float32)
    named = (column(names[0:1]) == lane_group) | (column(names[1:2]) == lane_group)
    chunks = []
    for d in range(4):
        arrived(SR.at[d], s_rcv.at[d])
        chunks.append(jnp.where(named, S[d, x] + SR[d], -jnp.inf))
    highest = jnp.maximum(jnp.maximum(chunks[0], chunks[1]), jnp.maximum(chunks[2], chunks[3]))
    highest = jnp.max(highest, axis=1, keepdims=True)
    spread = [jnp.exp(chunk - highest) for chunk in chunks]
    total = jnp.sum((spread[0] + spread[1]) + (spread[2] + spread[3]), axis=1, keepdims=True)
    normalizer = highest + jnp.log(total)
    norm[...] = jnp.broadcast_to(normalizer, norm.shape)
    even = lane_group % 2 == 0
    for p in halves:
        low = jnp.exp(chunks[2 * p] - normalizer)
        high = jnp.exp(chunks[2 * p + 1] - normalizer)
        zero = jnp.where(even, low, pltpu.roll(high, refs, 1))
        one = jnp.where(even, pltpu.roll(low, width - refs, 1), high)
        QP[p, c, x] = jnp.where(c == 0, zero, one).astype(jnp.bfloat16)
        QO[p] = jnp.where(c == 0, one, zero).astype(jnp.bfloat16)
    for k in (2, 0, 1):
        post_copy(k).start()

    @pl.when(is_end)
    def _():
        post_far(c, x).start()

    for i, j in ((1 - c, x), (c, 1 - x), (1 - c, 1 - x)):
        arrived(QP.at[:, i, j], q_rcv.at[i, j])

        @pl.when(is_end)
        def _():
            post_far(i, j).start()

    def turned(block):
        flat = block.reshape(4 * rows, width).astype(jnp.float32)
        return flat.T.astype(jnp.bfloat16)

    for p in halves:
        QT[p] = turned(QP[p])
    for i in range(2):
        arrived(X.at[1 - c, i], x_rcv.at[1 - c, i, 0])

    def product(left, right):
        return lax.dot_general(
            left.reshape(2 * width, 4 * rows), right.reshape(4 * rows, tile),
            (((1,), (0,)), ((), ())), preferred_element_type=jnp.float32,
        )

    def span(t):
        return pl.ds(pl.multiple_of(t * tile, tile), tile)

    def near(t):
        return product(QT[...], X[:, :, :, span(t)])

    def keep(t, value):
        PROD[t] = value.reshape(2, 2, 2, refs, tile)

    def own(t, d):
        return PROD[t, d // 2, :, d % 2]

    def f32(value):
        return value.astype(jnp.float32)

    @pl.when(is_end)
    def _():
        def send(t, carry):
            keep(t, near(t))
            for k, d in enumerate((far_inner, far_end, inner)):
                TE[k, t - TF] = own(t, d).astype(jnp.bfloat16)
                end_copy(k, t - TF).start()
            return carry

        def pass_on(t, carry):
            arrived(RI.at[t], i_rcv.at[t])
            out_x(RI, t).start()
            out_own(RI, t).start()
            return carry

        def finish(t, carry):
            arrived(RI.at[t], i_rcv.at[t])
            O[t] = (own(t, end) + f32(RI[t])).astype(jnp.bfloat16)
            out_x(O, t).start()
            out_own(O, t).start()
            return carry

        lax.fori_loop(TF, T, send, 0)
        lax.fori_loop(0, TF, pass_on, 0)
        lax.fori_loop(TF, T, finish, 0)

    @pl.when(is_inner)
    def _():
        for i in range(2):
            arrived(XF.at[c, i], xf_rcv.at[c, i])
            far_core(i).start()
        for i in range(2):
            arrived(XF.at[1 - c, i], xf_rcv.at[1 - c, i])
        for i in range(2):
            for j in range(2):
                arrived(QF.at[:, i, j], qf_rcv.at[i, j])
        for p in halves:
            QTF[p] = turned(QF[p])

        def outward(t, both):
            total = near(t)
            if both:
                total = total + product(QTF[...], XF[:, :, :, span(t)])
            keep(t, total)
            for k, d in enumerate((far_inner, far_end)):
                value = own(t, d)
                if not both:
                    arrived(RE.at[k, t - TF], e_rcv.at[k, t - TF])
                    value = value + f32(RE[k, t - TF])
                TM[k, t] = value.astype(jnp.bfloat16)
                middle_copy(k, t).start()

        def inward(t):
            arrived(RM.at[1, t], m_rcv.at[1, t])
            TI[t] = (own(t, end) + f32(RM[1, t])).astype(jnp.bfloat16)
            inner_copy(t).start()
            arrived(RM.at[0, t], m_rcv.at[0, t])

            @pl.when(t < TF)
            def _():
                O[t] = (own(t, inner) + f32(RM[0, t])).astype(jnp.bfloat16)

            @pl.when(t >= TF)
            def _():
                arrived(RE.at[2, t - TF], e_rcv.at[2, t - TF])
                O[t] = (own(t, inner) + f32(RM[0, t]) + f32(RE[2, t - TF])).astype(jnp.bfloat16)

            out_x(O, t).start()
            out_own(O, t).start()

        def first(t, carry):
            outward(t, True)

            @pl.when(t >= 2)
            def _():
                inward(t - 2)

            return carry

        def second(t, carry):
            outward(t, False)
            inward(t - 2)
            return carry

        def last(t, carry):
            inward(t)
            return carry

        lax.fori_loop(0, TF, first, 0)
        lax.fori_loop(TF, T, second, 0)
        lax.fori_loop(T - 2, T, last, 0)

    for h in halves:
        proj_x(h).wait_send()
        image_x(h).wait_send()
    own_image_core().wait_send()
    other_image_core().wait_send()
    for k in range(3):
        post_copy(k).wait_send()

    def sent(src, carry):
        score_copy(src).wait_send()
        for g, h in pieces:
            piece = part(src, g, h)
            to_core(piece, src, g, h).wait_send()

            @pl.when((src == b) | (is_inner & (src != buddy)))
            def _():
                to_buddy(piece, src, g, h).wait_send()

            @pl.when(is_inner & ((src == b) | (src == buddy)))
            def _():
                to_across(piece, src, g, h).wait_send()

        return carry

    lax.fori_loop(0, 4, sent, 0)

    @pl.when(is_end)
    def _():
        own_far().wait_send()
        other_far().wait_send()
        for i in range(2):
            for j in range(2):
                post_far(i, j).wait_send()

        def gone(t, carry):
            for k in range(3):
                end_copy(k, t).wait_send()
            return carry

        lax.fori_loop(0, T - TF, gone, 0)

    @pl.when(is_inner)
    def _():
        for i in range(2):
            far_core(i).wait_send()

        def gone(t, carry):
            for k in range(2):
                middle_copy(k, t).wait_send()
            inner_copy(t).wait_send()
            return carry

        lax.fori_loop(0, T, gone, 0)

    def done(t, carry):
        out_own(O, t).wait()
        out_x(O, t).wait_send()
        arrived(out_span(1 - x, t), o_rcv.at[t])
        return carry

    lax.fori_loop(0, T, done, 0)


def paired_halves(images, routes, projections, noise_weights):
    rows, coef = images.shape
    refs = projections.shape[1]
    H, width = coef // 2, 4 * refs
    F = H // 2
    tile = min(F, 512)
    T, TF = H // tile, F // tile
    TN = T - TF
    dma = pltpu.SemaphoreType.DMA
    bf16, f32 = jnp.bfloat16, jnp.float32
    piece = (2, refs, tile)
    sums, norm = pl.pallas_call(
        paired,
        out_shape=(
            jax.ShapeDtypeStruct((refs, coef), bf16),
            jax.ShapeDtypeStruct((rows, 128), f32),
        ),
        in_specs=[pl.BlockSpec(memory_space=pltpu.HBM)] * 4,
        out_specs=(
            pl.BlockSpec(memory_space=pl.ANY),
            pl.BlockSpec(memory_space=pltpu.VMEM),
        ),
        scratch_shapes=[
            pltpu.VMEM((2, rows), jnp.int32),
            pltpu.VMEM((H,), f32),
            pltpu.VMEM((2, 2, rows, H), bf16),
            pltpu.VMEM((2, 2, rows, F), bf16),
            pltpu.VMEM((4, 4, refs, H), bf16),
            pltpu.VMEM((4, 2, rows, width), f32),
            pltpu.VMEM((4, rows, width), f32),
            pltpu.VMEM((2, 2, 2, rows, width), bf16),
            pltpu.VMEM((2, rows, width), bf16),
            pltpu.VMEM((2, 2, 2, rows, width), bf16),
            pltpu.VMEM((2, width, 4 * rows), bf16),
            pltpu.VMEM((2, width, 4 * rows), bf16),
            pltpu.VMEM((T, 2, 2, 2, refs, tile), f32),
            pltpu.VMEM((3, TN) + piece, bf16),
            pltpu.VMEM((3, TN) + piece, bf16),
            pltpu.VMEM((2, T) + piece, bf16),
            pltpu.VMEM((2, T) + piece, bf16),
            pltpu.VMEM((T,) + piece, bf16),
            pltpu.VMEM((T,) + piece, bf16),
            pltpu.VMEM((T,) + piece, bf16),
            dma((4,)), dma((2,)), dma((4, 4, 2)), dma((4, 4, 2)), dma((4, 4, 2)), dma((4, 4, 2)),
            dma((2,)), dma((2,)), dma((2, 2, 2)), dma((2,)), dma((2,)), dma((2, 2)),
            dma((4,)), dma((4,)), dma((3,)), dma((2, 2)), dma((2, 2)), dma((2, 2)),
            dma((3, TN)), dma((3, TN)), dma((2, T)), dma((2, T)), dma((T,)), dma((T,)),
            dma((T,)), dma((T,)), dma((T,)),
        ],
        compiler_params=pltpu.CompilerParams(
            collective_id=0, has_side_effects=True, vmem_limit_bytes=64 * 1024 * 1024 - 65536
        ),
        cost_estimate=pl.CostEstimate(
            flops=4 * 4 * rows * 4 * width * H // 2, bytes_accessed=4 * rows * coef, transcendentals=0
        ),
    )(images, routes.T, projections[0], noise_weights)
    return (sums.astype(f32)[None], norm[:, 0])


def solution(mesh):
    sizes = dict(mesh.shape)
    direct = sizes["sub"] == 1 and sizes["reader"] == 4 and sizes["blk"] == 4
    return jax.shard_map(
        paired_halves if direct else routed,
        mesh=mesh,
        in_specs=(
            P(("parts", "blk", "reader"), "sub"),
            P(("parts", "blk", "reader"), None),
            P(("parts", "reader"), "blk", "sub"),
            P(("parts", "sub")),
        ),
        out_specs=(P(("parts", "reader"), "blk", "sub"), P(("parts", "blk", "reader"))),
        check_vma=False,
    )
```

time: 91.3 us -> 89.1 us (0.976)
  the two profiles are of different devices: /device:TPU:16 before, /device:TPU:0 now
where the time goes in v1:
time: 89.1 us; the launch traced here: 88.9 us
  Pallas kernels  84.7 us (95%)
  other arithmetic  2.08 us (2%)
  local copies, waits for them, and re-layouts  1.43 us (2%)
    pallas_call x1, Pallas kernels, paired_halves(): pl.pallas_call(paired, out_shape=(jax.ShapeDtypeStruct((refs, coef), bf16...  84.7 us
    broadcast_in_dim x1, other arithmetic, paired_halves(): return (sums.astype(f32)[None], norm[:, 0])  2.08 us

profile of v1, /device:TPU:0, one launch (start us, length us, event | category | flops | bytes accessed | tf_op | source)
XLA Modules:
  0.0 88.9 jit_solution(9852511455421029525)
XLA Ops:
  0.6 84.7 %shard_map.59 = (bf16[32,8192]{1,0:T(8,128)(2,1)}, f32[96,128]{1,0:T(8,128)}) custom-call(bf16[96,8192]{1,0:T(8,128)(2,1)} %images.1, s32[2,96]{1,0:T(2,128)} %bitcast.6, bf16[32,8192]{1,0:T(8,128)(2,1)} %bitcast.5, f32[8192]{0:T(1024)} %noise_in.1), custom_call_target="tpu_custom_call" | custom-call | flops 1610612736 | bytes 3145728 | tf_op jit(solution)/shard_map/pallas_call | solution.py:610
  85.4 1.4 %slice_reduce_fusion = f32[96]{0:T(128)} fusion(f32[96,128]{1,0:T(8,128)} %get-tuple-element.5), kind=kLoop, calls=%fused_computation.1 | loop fusion | bytes 768 | tf_op jit(solution)/shard_map/slice | solution.py:655
  86.8 2.1 %bitcast_convert_fusion = f32[1,32,8192]{2,1,0:T(8,128)} fusion(bf16[32,8192]{1,0:T(8,128)(2,1)} %get-tuple-element.4), kind=kLoop, calls=%fused_computation | loop fusion | flops 262144 | bytes 1572864 | tf_op jit(solution)/shard_map/broadcast_in_dim | solution.py:655

commit v2 on v1

--- a/solution.py
+++ b/solution.py
@@ -125,9 +125,9 @@
 def paired(
     images, routes_in, proj, noise_in,
     out, norm,
-    routes, noise, X, XF, PR, S, SR, QP, QO, QF, QT, QTF, PROD, TE, RE, TM, RM, TI, RI, O,
+    routes, noise, X, XF, PR, S, SR, SF, FR, QP, QO, QF, QT, QTF, PROD, TE, RE, TM, RM, TI, RI, O,
     loc, px_snd, pb_snd, pm_snd, pc_snd, p_rcv, xx_snd, xc_snd, x_rcv, xf_snd, xfc_snd, xf_rcv,
-    s_snd, s_rcv, q_snd, q_rcv, qf_snd, qf_rcv, e_snd, e_rcv, m_snd, m_rcv, i_snd, i_rcv,
+    s_snd, s_rcv, f_snd, f_rcv, q_snd, q_rcv, qf_snd, qf_rcv, e_snd, e_rcv, m_snd, m_rcv, i_snd, i_rcv,
     own_snd, o_snd, o_rcv,
 ):
     r = lax.axis_index("reader")
@@ -147,8 +147,14 @@
     F = H // 2
     T, tile = O.shape[0], O.shape[3]
     TF = F // tile
+    cuts = score_cuts(T)
+    low, mid = (n * tile for n in cuts)
     width = 4 * refs
     halves = (0, 1)
+    whole = ((0, mid), (mid, H - mid))
+    short = ((low, mid - low), (mid, H - mid))
+    strips = ((0, low), (low, H - low))
+    far_strips = ((0, low), (low, F - low))
 
     def remote(src, dst, snd, rcv, **where):
         return pltpu.make_async_remote_copy(
@@ -159,30 +165,32 @@
     def arrived(dst, sem):
         remote(dst, dst, sem, sem, reader=rx).wait_recv()
 
-    def columns(i, h):
-        return pl.ds(pl.multiple_of(i * H + h * F, F), F)
-
-    def part(src, g, h):
-        return PR.at[src, g, :, pl.ds(h * F, F)]
+    def columns(i, cut):
+        return pl.ds(pl.multiple_of(i * H + cut[0], tile), cut[1])
+
+    def part(src, g, cut):
+        return PR.at[src, g, :, pl.ds(*cut)]
 
     def own_piece(h):
-        return proj.at[:, columns(x, h)]
+        return proj.at[:, columns(x, whole[h])]
 
     def proj_x(h):
-        return remote(proj.at[:, columns(1 - x, h)], part(b, r, h), px_snd.at[h], p_rcv.at[b, r, h], reader=rx)
-
-    def to_core(piece, src, g, h):
-        return remote(piece, part(src, g, h), pc_snd.at[src, g, h], p_rcv.at[src, g, h], reader=rc)
-
-    def to_buddy(piece, src, g, h):
-        return remote(piece, part(src, g, h), pb_snd.at[src, g, h], p_rcv.at[src, g, h], blk=buddy)
+        return remote(
+            proj.at[:, columns(1 - x, whole[h])], part(b, r, whole[h]), px_snd.at[h], p_rcv.at[b, r, h], reader=rx
+        )
+
+    def to_core(piece, src, g, h, cut):
+        return remote(piece, part(src, g, cut), pc_snd.at[src, g, h], p_rcv.at[src, g, h], reader=rc)
+
+    def to_buddy(piece, src, g, h, cut):
+        return remote(piece, part(src, g, cut), pb_snd.at[src, g, h], p_rcv.at[src, g, h], blk=buddy)
 
     def to_across(piece, src, g, h):
-        return remote(piece, part(src, g, h), pm_snd.at[src, g, h], p_rcv.at[src, g, h], blk=across)
+        return remote(piece, part(src, g, whole[h]), pm_snd.at[src, g, h], p_rcv.at[src, g, h], blk=across)
 
     def image_x(h):
         return remote(
-            images.at[:, columns(1 - x, h)], X.at[c, x, :, pl.ds(h * F, F)],
+            images.at[:, columns(1 - x, strips[h])], X.at[c, x, :, pl.ds(*strips[h])],
             xx_snd.at[h], x_rcv.at[c, x, h], reader=rx,
         )
 
@@ -195,19 +203,28 @@
     def other_image_core():
         return remote(X.at[c, 1 - x], X.at[c, 1 - x], xc_snd.at[1], x_rcv.at[c, 1 - x, 0], reader=rc)
 
-    def own_far():
-        return remote(images.at[:, columns(x, 0)], XF.at[c, x], xf_snd.at[0], xf_rcv.at[c, x], blk=buddy)
-
-    def other_far():
+    def own_far(h):
         return remote(
-            X.at[c, 1 - x, :, pl.ds(0, F)], XF.at[c, 1 - x], xf_snd.at[1], xf_rcv.at[c, 1 - x], blk=buddy
+            images.at[:, columns(x, far_strips[h])], XF.at[c, x, :, pl.ds(*far_strips[h])],
+            xf_snd.at[0, h], xf_rcv.at[c, x, h], blk=buddy,
+        )
+
+    def other_far(h):
+        return remote(
+            X.at[c, 1 - x, :, pl.ds(*far_strips[h])], XF.at[c, 1 - x, :, pl.ds(*far_strips[h])],
+            xf_snd.at[1, h], xf_rcv.at[c, 1 - x, h], blk=buddy,
         )
 
     def far_core(i):
-        return remote(XF.at[c, i], XF.at[c, i], xfc_snd.at[i], xf_rcv.at[c, i], reader=rc)
+        return remote(XF.at[c, i], XF.at[c, i], xfc_snd.at[i], xf_rcv.at[c, i, 0], reader=rc)
 
     def score_copy(src):
         return remote(S.at[src, 1 - x], SR.at[src], s_snd.at[src], s_rcv.at[src], reader=rx)
+
+    def far_score(k, i):
+        if i == 0:
+            return remote(SF.at[k, x], FR.at[k, x], f_snd.at[k, 0], f_rcv.at[k, x], blk=buddy)
+        return remote(SF.at[k, 1 - x], FR.at[k, x], f_snd.at[k, 1], f_rcv.at[k, x], blk=buddy, reader=rx)
 
     def post_copy(k):
         source, to = ((QP.at[:, c, x], rx), (QO, rc), (QO, rd))[k]
@@ -247,6 +264,7 @@
     for k in (rx, rc, rd):
         pl.semaphore_signal(barrier, inc=1, device_id={"reader": k}, device_id_type=MESH)
     pl.semaphore_signal(barrier, inc=1, device_id={"blk": buddy}, device_id_type=MESH)
+    pl.semaphore_signal(barrier, inc=1, device_id={"blk": buddy, "reader": rx}, device_id_type=MESH)
 
     @pl.when(is_inner)
     def _():
@@ -256,64 +274,66 @@
     own_image.start()
     noise_copy.start()
     routes_copy.start()
-    pl.semaphore_wait(barrier, 4 + is_inner.astype(jnp.int32))
+    pl.semaphore_wait(barrier, 5 + is_inner.astype(jnp.int32))
 
     for h in halves:
         proj_x(h).start()
-        to_buddy(own_piece(h), b, r, h).start()
+        to_buddy(own_piece(h), b, r, h, whole[h]).start()
 
         @pl.when(is_inner)
         def _():
             to_across(own_piece(h), b, r, h).start()
 
     for h in halves:
-        to_core(own_piece(h), b, r, h).start()
+        to_core(own_piece(h), b, r, h, whole[h]).start()
     own_image_core().start()
     for h in halves:
-        piece = part(b, rx, h)
+        piece = part(b, rx, whole[h])
         arrived(piece, p_rcv.at[b, rx, h])
-        to_buddy(piece, b, rx, h).start()
+        to_buddy(piece, b, rx, h, whole[h]).start()
 
         @pl.when(is_inner)
         def _():
             to_across(piece, b, rx, h).start()
 
         image_x(h).start()
-        to_core(piece, b, rx, h).start()
+        to_core(piece, b, rx, h, whole[h]).start()
 
     pieces = ((r, 0), (r, 1), (rx, 0), (rx, 1))
 
+    def other_image(h):
+        arrived(X.at[c, 1 - x, :, pl.ds(*strips[h])], x_rcv.at[c, 1 - x, h])
+
+    def hand_over(src, g, h, cut):
+        piece = part(src, g, cut)
+        arrived(piece, p_rcv.at[src, g, h])
+        to_core(piece, src, g, h, cut).start()
+
     @pl.when(is_end)
     def _():
-        own_far().start()
+        own_far(0).start()
         for g, h in pieces:
-            arrived(part(buddy, g, h), p_rcv.at[buddy, g, h])
-            to_core(part(buddy, g, h), buddy, g, h).start()
-        arrived(X.at[c, 1 - x, :, pl.ds(0, F)], x_rcv.at[c, 1 - x, 0])
-        other_far().start()
+            hand_over(buddy, g, h, whole[h])
+        other_image(0)
+        other_far(0).start()
+        own_far(1).start()
         for g, h in pieces:
-            arrived(part(far_inner, g, h), p_rcv.at[far_inner, g, h])
-            to_core(part(far_inner, g, h), far_inner, g, h).start()
-        arrived(X.at[c, 1 - x, :, pl.ds(F, F)], x_rcv.at[c, 1 - x, 1])
+            hand_over(far_inner, g, h, short[h])
+        other_image(1)
+        other_far(1).start()
 
     @pl.when(is_inner)
     def _():
         for g, h in pieces:
-            piece = part(buddy, g, h)
-            arrived(piece, p_rcv.at[buddy, g, h])
-            to_across(piece, buddy, g, h).start()
-            to_core(piece, buddy, g, h).start()
-            piece = part(far_inner, g, h)
-            arrived(piece, p_rcv.at[far_inner, g, h])
-            to_buddy(piece, far_inner, g, h).start()
-            to_core(piece, far_inner, g, h).start()
+            hand_over(buddy, g, h, whole[h])
+            to_across(part(buddy, g, whole[h]), buddy, g, h).start()
+            hand_over(far_inner, g, h, whole[h])
+            to_buddy(part(far_inner, g, short[h]), far_inner, g, h, short[h]).start()
         for g, h in pieces:
-            piece = part(far_end, g, h)
-            arrived(piece, p_rcv.at[far_end, g, h])
-            to_buddy(piece, far_end, g, h).start()
-            to_core(piece, far_end, g, h).start()
+            hand_over(far_end, g, h, whole[h])
+            to_buddy(part(far_end, g, short[h]), far_end, g, h, short[h]).start()
         for h in halves:
-            arrived(X.at[c, 1 - x, :, pl.ds(h * F, F)], x_rcv.at[c, 1 - x, h])
+            other_image(h)
 
     other_image_core().start()
     own_proj.wait()
@@ -321,15 +341,15 @@
     noise_copy.wait()
     routes_copy.wait()
 
-    def score_half(src, h):
+    def scores_of(block, src, tiles):
         scores = jnp.zeros((2 * rows, width), jnp.float32)
         penalty = jnp.zeros((width, 128), jnp.float32)
-        for t in range(TF):
-            cut = pl.ds(h * F + t * tile, tile)
+        for t in tiles:
+            cut = pl.ds(t * tile, tile)
             refs_f = PR[src, :, :, cut].reshape(width, tile).astype(jnp.float32)
             scaled = refs_f * noise[cut][None, :]
             scores = scores + lax.dot_general(
-                X[c, :, :, cut].reshape(2 * rows, tile), scaled.astype(jnp.bfloat16),
+                block[c, :, :, cut].reshape(2 * rows, tile), scaled.astype(jnp.bfloat16),
                 (((1,), (1,)), ((), ())), preferred_element_type=jnp.float32,
             )
             squares = scaled * refs_f
@@ -340,33 +360,73 @@
             (((1,), (1,)), ((), ())), preferred_element_type=jnp.float32,
             precision=lax.Precision.HIGHEST,
         )
-        scores = (scores - penalty_row[0:1]).reshape(2, rows, width)
-        S[src] = scores if h == 0 else S[src] + scores
-
-    def from_core(src, h):
+        return (scores - penalty_row[0:1]).reshape(2, rows, width)
+
+    def from_core(src, h, cut):
         for g in (rc, rd):
-            arrived(part(src, g, h), p_rcv.at[src, g, h])
+            arrived(part(src, g, cut), p_rcv.at[src, g, h])
+
+    @pl.when(is_inner)
+    def _():
+        for i in (x, 1 - x):
+            arrived(XF.at[c, i, :, pl.ds(*far_strips[0])], xf_rcv.at[c, i, 0])
+
+        def far_source(k, carry):
+            src = jnp.where(k == 0, far_inner, far_end)
+            for h in halves:
+                from_core(src, h, whole[h])
+            SF[k] = scores_of(XF, src, range(cuts[0]))
+            for i in (1, 0):
+                far_score(k, i).start()
+            return carry
+
+        lax.fori_loop(0, 2, far_source, 0)
 
     def score_source(i, carry):
-        src = jnp.where(i == 0, b, jnp.where(i == 1, buddy, far_inner))
-        for h in halves:
-            from_core(src, h)
-            score_half(src, h)
+        src = jnp.where(i == 0, b, jnp.where(i == 1, buddy, jnp.where(i == 2, far_inner, far_end)))
+
+        @pl.when(i < 2)
+        def _():
+            for h in halves:
+                from_core(src, h, whole[h])
+
+        @pl.when((i < 2) | is_inner)
+        def _():
+            S[src] = scores_of(X, src, range(cuts[0]))
+
+        @pl.when((i >= 2) & is_end)
+        def _():
+            @pl.when(i == 3)
+            def _():
+                for g, h in pieces[:3]:
+                    hand_over(src, g, h, short[h])
+
+            from_core(src, 0, short[0])
+            S[src] = jnp.zeros((2, rows, width), jnp.float32)
+
+        S[src] = S[src] + scores_of(X, src, range(cuts[0], cuts[1]))
+
+        @pl.when((i >= 2) & is_end)
+        def _():
+            @pl.when(i == 3)
+            def _():
+                for g, h in pieces[3:]:
+                    hand_over(src, g, h, short[h])
+
+            from_core(src, 1, short[1])
+
+        S[src] = S[src] + scores_of(X, src, range(cuts[1], T))
         score_copy(src).start()
         return carry
 
-    lax.fori_loop(0, 3, score_source, 0)
-    for h in halves:
-        @pl.when(is_end)
-        def _():
-            for g, k in (pieces[:3], pieces[3:])[h]:
-                piece = part(far_end, g, k)
-                arrived(piece, p_rcv.at[far_end, g, k])
-                to_core(piece, far_end, g, k).start()
-
-        from_core(far_end, h)
-        score_half(far_end, h)
-    score_copy(far_end).start()
+    lax.fori_loop(0, 4, score_source, 0)
+
+    @pl.when(is_end)
+    def _():
+        for k, src in enumerate((far_inner, far_end)):
+            for i in range(2):
+                arrived(FR.at[k, i], f_rcv.at[k, i])
+            S[src, x] = S[src, x] + FR[k, 0] + FR[k, 1]
 
     lane = lax.broadcasted_iota(jnp.int32, (rows, width), 1)
     lane_group = lane // refs
@@ -388,7 +448,7 @@
     spread = [jnp.exp(chunk - highest) for chunk in chunks]
     total = jnp.sum((spread[0] + spread[1]) + (spread[2] + spread[3]), axis=1, keepdims=True)
     normalizer = highest + jnp.log(total)
-    norm[...] = jnp.broadcast_to(normalizer, norm.shape)
+    norm[...] = jnp.sum(jnp.where(diagonal, normalizer, 0.0), axis=0, keepdims=True)
     even = lane_group % 2 == 0
     for p in halves:
         low = jnp.exp(chunks[2 * p] - normalizer)
@@ -404,6 +464,45 @@
     def _():
         post_far(c, x).start()
 
+    for h in halves:
+        proj_x(h).wait_send()
+        image_x(h).wait_send()
+    own_image_core().wait_send()
+    other_image_core().wait_send()
+
+    def sent(src, carry):
+        score_copy(src).wait_send()
+        near_source = (src == b) | (src == buddy)
+        for g, h in pieces:
+            @pl.when(near_source | is_inner)
+            def _():
+                piece = part(src, g, whole[h])
+                to_core(piece, src, g, h, whole[h]).wait_send()
+
+            @pl.when(src == b)
+            def _():
+                piece = part(src, g, whole[h])
+                to_buddy(piece, src, g, h, whole[h]).wait_send()
+
+            @pl.when((src != b) & (src != buddy))
+            def _():
+                piece = part(src, g, short[h])
+
+                @pl.when(is_inner)
+                def _():
+                    to_buddy(piece, src, g, h, short[h]).wait_send()
+
+                @pl.when(is_end)
+                def _():
+                    to_core(piece, src, g, h, short[h]).wait_send()
+
+            @pl.when(is_inner & near_source)
+            def _():
+                to_across(part(src, g, whole[h]), src, g, h).wait_send()
+
+        return carry
+
+    lax.fori_loop(0, 4, sent, 0)
     for i, j in ((1 - c, x), (c, 1 - x), (1 - c, 1 - x)):
         arrived(QP.at[:, i, j], q_rcv.at[i, j])
 
@@ -445,7 +544,7 @@
     def _():
         def send(t, carry):
             keep(t, near(t))
-            for k, d in enumerate((far_inner, far_end, inner)):
+            for k, d in ((1, far_end), (0, far_inner), (2, inner)):
                 TE[k, t - TF] = own(t, d).astype(jnp.bfloat16)
                 end_copy(k, t - TF).start()
             return carry
@@ -470,99 +569,79 @@
     @pl.when(is_inner)
     def _():
         for i in range(2):
-            arrived(XF.at[c, i], xf_rcv.at[c, i])
+            arrived(XF.at[c, i, :, pl.ds(*far_strips[1])], xf_rcv.at[c, i, 1])
             far_core(i).start()
         for i in range(2):
-            arrived(XF.at[1 - c, i], xf_rcv.at[1 - c, i])
+            arrived(XF.at[1 - c, i], xf_rcv.at[1 - c, i, 0])
         for i in range(2):
             for j in range(2):
                 arrived(QF.at[:, i, j], qf_rcv.at[i, j])
         for p in halves:
             QTF[p] = turned(QF[p])
 
-        def outward(t, both):
-            total = near(t)
-            if both:
-                total = total + product(QTF[...], XF[:, :, :, span(t)])
-            keep(t, total)
-            for k, d in enumerate((far_inner, far_end)):
-                value = own(t, d)
-                if not both:
-                    arrived(RE.at[k, t - TF], e_rcv.at[k, t - TF])
-                    value = value + f32(RE[k, t - TF])
-                TM[k, t] = value.astype(jnp.bfloat16)
-                middle_copy(k, t).start()
-
-        def inward(t):
-            arrived(RM.at[1, t], m_rcv.at[1, t])
-            TI[t] = (own(t, end) + f32(RM[1, t])).astype(jnp.bfloat16)
-            inner_copy(t).start()
-            arrived(RM.at[0, t], m_rcv.at[0, t])
-
+        def outward(k, d, t):
             @pl.when(t < TF)
             def _():
-                O[t] = (own(t, inner) + f32(RM[0, t])).astype(jnp.bfloat16)
+                TM[k, t] = own(t, d).astype(jnp.bfloat16)
 
             @pl.when(t >= TF)
             def _():
-                arrived(RE.at[2, t - TF], e_rcv.at[2, t - TF])
-                O[t] = (own(t, inner) + f32(RM[0, t]) + f32(RE[2, t - TF])).astype(jnp.bfloat16)
-
-            out_x(O, t).start()
-            out_own(O, t).start()
-
-        def first(t, carry):
-            outward(t, True)
-
-            @pl.when(t >= 2)
-            def _():
-                inward(t - 2)
+                arrived(RE.at[k, t - TF], e_rcv.at[k, t - TF])
+                TM[k, t] = (own(t, d) + f32(RE[k, t - TF])).astype(jnp.bfloat16)
+
+            middle_copy(k, t).start()
+
+        def turn(t, carry):
+            @pl.when(t < TF)
+            def _():
+                keep(t, near(t) + product(QTF[...], XF[:, :, :, span(t)]))
+
+            @pl.when((t >= TF) & (t < T))
+            def _():
+                keep(t, near(t))
+
+            @pl.when(t < T)
+            def _():
+                outward(1, far_end, t)
+
+            @pl.when((t >= 2) & (t < T + 2))
+            def _():
+                outward(0, far_inner, t - 2)
+                n = t - 2
+                arrived(RM.at[1, n], m_rcv.at[1, n])
+                TI[n] = (own(n, end) + f32(RM[1, n])).astype(jnp.bfloat16)
+                inner_copy(n).start()
+
+            @pl.when(t >= 4)
+            def _():
+                n = t - 4
+                arrived(RM.at[0, n], m_rcv.at[0, n])
+                total = own(n, inner) + f32(RM[0, n])
+
+                @pl.when(n < TF)
+                def _():
+                    O[n] = total.astype(jnp.bfloat16)
+
+                @pl.when(n >= TF)
+                def _():
+                    arrived(RE.at[2, n - TF], e_rcv.at[2, n - TF])
+                    O[n] = (total + f32(RE[2, n - TF])).astype(jnp.bfloat16)
+
+                out_x(O, n).start()
+                out_own(O, n).start()
 
             return carry
 
-        def second(t, carry):
-            outward(t, False)
-            inward(t - 2)
-            return carry
-
-        def last(t, carry):
-            inward(t)
-            return carry
-
-        lax.fori_loop(0, TF, first, 0)
-        lax.fori_loop(TF, T, second, 0)
-        lax.fori_loop(T - 2, T, last, 0)
-
-    for h in halves:
-        proj_x(h).wait_send()
-        image_x(h).wait_send()
-    own_image_core().wait_send()
-    other_image_core().wait_send()
+        lax.fori_loop(0, T + 4, turn, 0)
+
     for k in range(3):
         post_copy(k).wait_send()
 
-    def sent(src, carry):
-        score_copy(src).wait_send()
-        for g, h in pieces:
-            piece = part(src, g, h)
-            to_core(piece, src, g, h).wait_send()
-
-            @pl.when((src == b) | (is_inner & (src != buddy)))
-            def _():
-                to_buddy(piece, src, g, h).wait_send()
-
-            @pl.when(is_inner & ((src == b) | (src == buddy)))
-            def _():
-                to_across(piece, src, g, h).wait_send()
-
-        return carry
-
-    lax.fori_loop(0, 4, sent, 0)
-
     @pl.when(is_end)
     def _():
-        own_far().wait_send()
-        other_far().wait_send()
+        for h in halves:
+            own_far(h).wait_send()
+            other_far(h).wait_send()
         for i in range(2):
             for j in range(2):
                 post_far(i, j).wait_send()
@@ -578,6 +657,8 @@
     def _():
         for i in range(2):
             far_core(i).wait_send()
+            for k in range(2):
+                far_score(k, i).wait_send()
 
         def gone(t, carry):
             for k in range(2):
@@ -594,6 +675,16 @@
         return carry
 
     lax.fori_loop(0, T, done, 0)
+
+
+def score_cuts(T):
+    low = max(1, 3 * T // 8)
+    return low, max(low + 1, 3 * T // 4)
+
+
+def hand_out(sums_in, norm_in, sums_out, norm_out):
+    sums_out[...] = sums_in[...].astype(jnp.float32)
+    norm_out[...] = norm_in[...]
 
 
 def paired_halves(images, routes, projections, noise_weights):
@@ -611,7 +702,7 @@
         paired,
         out_shape=(
             jax.ShapeDtypeStruct((refs, coef), bf16),
-            jax.ShapeDtypeStruct((rows, 128), f32),
+            jax.ShapeDtypeStruct((1, rows), f32),
         ),
         in_specs=[pl.BlockSpec(memory_space=pltpu.HBM)] * 4,
         out_specs=(
@@ -626,6 +717,8 @@
             pltpu.VMEM((4, 4, refs, H), bf16),
             pltpu.VMEM((4, 2, rows, width), f32),
             pltpu.VMEM((4, rows, width), f32),
+            pltpu.VMEM((2, 2, rows, width), f32),
+            pltpu.VMEM((2, 2, rows, width), f32),
             pltpu.VMEM((2, 2, 2, rows, width), bf16),
             pltpu.VMEM((2, rows, width), bf16),
             pltpu.VMEM((2, 2, 2, rows, width), bf16),
@@ -640,8 +733,8 @@
             pltpu.VMEM((T,) + piece, bf16),
             pltpu.VMEM((T,) + piece, bf16),
             dma((4,)), dma((2,)), dma((4, 4, 2)), dma((4, 4, 2)), dma((4, 4, 2)), dma((4, 4, 2)),
-            dma((2,)), dma((2,)), dma((2, 2, 2)), dma((2,)), dma((2,)), dma((2, 2)),
-            dma((4,)), dma((4,)), dma((3,)), dma((2, 2)), dma((2, 2)), dma((2, 2)),
+            dma((2,)), dma((2,)), dma((2, 2, 2)), dma((2, 2)), dma((2,)), dma((2, 2, 2)),
+            dma((4,)), dma((4,)), dma((2, 2)), dma((2, 2)), dma((3,)), dma((2, 2)), dma((2, 2)), dma((2, 2)),
             dma((3, TN)), dma((3, TN)), dma((2, T)), dma((2, T)), dma((T,)), dma((T,)),
             dma((T,)), dma((T,)), dma((T,)),
         ],
@@ -652,7 +745,15 @@
             flops=4 * 4 * rows * 4 * width * H // 2, bytes_accessed=4 * rows * coef, transcendentals=0
         ),
     )(images, routes.T, projections[0], noise_weights)
-    return (sums.astype(f32)[None], norm[:, 0])
+    block = 2048 if coef % 2048 == 0 else coef
+    sums, norm = pl.pallas_call(
+        hand_out,
+        grid=(coef // block,),
+        out_shape=(jax.ShapeDtypeStruct((refs, coef), f32), jax.ShapeDtypeStruct((1, rows), f32)),
+        in_specs=[pl.BlockSpec((refs, block), lambda i: (0, i)), pl.BlockSpec((1, rows), lambda i: (0, 0))],
+        out_specs=(pl.BlockSpec((refs, block), lambda i: (0, i)), pl.BlockSpec((1, rows), lambda i: (0, 0))),
+    )(sums, norm)
+    return (sums[None], norm[0])
 
 
 def solution(mesh):

time: 89.1 us -> 83.4 us (0.936)
  Pallas kernels: 84.7 us -> 82.6 us
  other arithmetic: 2.08 us -> 0 us
  local copies, waits for them, and re-layouts: 1.43 us -> 0 us
    pallas_call x1, Pallas kernels: 84.7 us -> 79.3 us  [paired_halves(): pl.pallas_call(paired, out_shape=(jax.ShapeDtypeStruct((refs, coef), bf16...]
    pallas_call x0 -> x1, Pallas kernels: none -> 3.28 us  [paired_halves(): pl.pallas_call(hand_out, grid=(coef // block,), out_shape=(jax.ShapeDtype...]
    broadcast_in_dim x1 -> x0, other arithmetic: 2.08 us -> none  [paired_halves(): return (sums.astype(f32)[None], norm[:, 0])]
    slice x1 -> x0, local copies, waits for them, and re-layouts: 1.43 us -> none  [paired_halves(): return (sums.astype(f32)[None], norm[:, 0])]
where the time goes in v2:
time: 83.4 us; the launch traced here: 83.2 us
  Pallas kernels  82.6 us (99%)
    pallas_call x1, Pallas kernels, paired_halves(): pl.pallas_call(paired, out_shape=(jax.ShapeDtypeStruct((refs, coef), bf16...  79.3 us
    pallas_call x1, Pallas kernels, paired_halves(): pl.pallas_call(hand_out, grid=(coef // block,), out_shape=(jax.ShapeDtype...  3.28 us

profile of v2, /device:TPU:0, one launch (start us, length us, event | category | flops | bytes accessed | tf_op | source)
XLA Modules:
  0.0 83.2 jit_solution(819130459412140458)
XLA Ops:
  0.6 79.3 %shard_map.59 = (bf16[32,8192]{1,0:T(8,128)(2,1)}, f32[1,96]{1,0:T(1,128)}) custom-call(bf16[96,8192]{1,0:T(8,128)(2,1)} %images.1, s32[2,96]{1,0:T(2,128)} %bitcast.6, bf16[32,8192]{1,0:T(8,128)(2,1)} %bitcast.5, f32[8192]{0:T(1024)} %noise_in.1), custom_call_target="tpu_custom_call" | custom-call | flops 1610612736 | bytes 3145728 | tf_op jit(solution)/shard_map/pallas_call | solution.py:701
  79.9 3.3 %shard_map.60 = (f32[32,8192]{1,0:T(8,128)}, f32[1,96]{1,0:T(1,128)}) custom-call(bf16[32,8192]{1,0:T(8,128)(2,1)} %get-tuple-element.6.sums_in, f32[1,96]{1,0:T(1,128)} %get-tuple-element.7.norm_in), custom_call_target="tpu_custom_call" | custom-call | tf_op jit(solution)/shard_map/pallas_call | solution.py:749

commit v3 on v2

--- a/solution.py
+++ b/solution.py
@@ -226,12 +226,12 @@
             return remote(SF.at[k, x], FR.at[k, x], f_snd.at[k, 0], f_rcv.at[k, x], blk=buddy)
         return remote(SF.at[k, 1 - x], FR.at[k, x], f_snd.at[k, 1], f_rcv.at[k, x], blk=buddy, reader=rx)
 
-    def post_copy(k):
-        source, to = ((QP.at[:, c, x], rx), (QO, rc), (QO, rd))[k]
-        return remote(source, QP.at[:, c, x], q_snd.at[k], q_rcv.at[c, x], reader=to)
-
-    def post_far(i, j):
-        return remote(QP.at[:, i, j], QF.at[:, i, j], qf_snd.at[i, j], qf_rcv.at[i, j], blk=buddy)
+    def post_copy(k, p):
+        source, to = ((QP.at[p, c, x], rx), (QO.at[p], rc), (QO.at[p], rd))[k]
+        return remote(source, QP.at[p, c, x], q_snd.at[k, p], q_rcv.at[c, x, p], reader=to)
+
+    def post_far(i, j, p):
+        return remote(QP.at[p, i, j], QF.at[p, i, j], qf_snd.at[i, j, p], qf_rcv.at[i, j, p], blk=buddy)
 
     def end_copy(k, t):
         return remote(TE.at[k, t], RE.at[k, t], e_snd.at[k, t], e_rcv.at[k, t], blk=buddy)
@@ -316,11 +316,11 @@
             hand_over(buddy, g, h, whole[h])
         other_image(0)
         other_far(0).start()
-        own_far(1).start()
         for g, h in pieces:
             hand_over(far_inner, g, h, short[h])
         other_image(1)
-        other_far(1).start()
+        for g, h in pieces[:3]:
+            hand_over(far_end, g, h, short[h])
 
     @pl.when(is_inner)
     def _():
@@ -340,6 +340,10 @@
     own_image.wait()
     noise_copy.wait()
     routes_copy.wait()
+
+    square = lax.broadcasted_iota(jnp.int32, (width, width), 0) == lax.broadcasted_iota(
+        jnp.int32, (width, width), 1
+    )
 
     def scores_of(block, src, tiles):
         scores = jnp.zeros((2 * rows, width), jnp.float32)
@@ -355,12 +359,9 @@
             squares = scaled * refs_f
             for lane in range(0, tile, 128):
                 penalty = penalty + squares[:, lane : lane + 128]
-        penalty_row = lax.dot_general(
-            jnp.full((8, 128), 0.5, jnp.float32), penalty,
-            (((1,), (1,)), ((), ())), preferred_element_type=jnp.float32,
-            precision=lax.Precision.HIGHEST,
-        )
-        return (scores - penalty_row[0:1]).reshape(2, rows, width)
+        lanes = jnp.sum(penalty, axis=1, keepdims=True)
+        penalty_row = 0.5 * jnp.sum(jnp.where(square, lanes, 0.0), axis=0, keepdims=True)
+        return (scores - penalty_row).reshape(2, rows, width)
 
     def from_core(src, h, cut):
         for g in (rc, rd):
@@ -392,30 +393,21 @@
 
         @pl.when((i < 2) | is_inner)
         def _():
-            S[src] = scores_of(X, src, range(cuts[0]))
+            S[src] = scores_of(X, src, range(T))
 
         @pl.when((i >= 2) & is_end)
         def _():
-            @pl.when(i == 3)
-            def _():
-                for g, h in pieces[:3]:
-                    hand_over(src, g, h, short[h])
-
             from_core(src, 0, short[0])
-            S[src] = jnp.zeros((2, rows, width), jnp.float32)
-
-        S[src] = S[src] + scores_of(X, src, range(cuts[0], cuts[1]))
-
-        @pl.when((i >= 2) & is_end)
-        def _():
+            S[src] = scores_of(X, src, range(cuts[0], cuts[1]))
+
             @pl.when(i == 3)
             def _():
                 for g, h in pieces[3:]:
                     hand_over(src, g, h, short[h])
 
             from_core(src, 1, short[1])
-
-        S[src] = S[src] + scores_of(X, src, range(cuts[1], T))
+            S[src] = S[src] + scores_of(X, src, range(cuts[1], T))
+
         score_copy(src).start()
         return carry
 
@@ -423,6 +415,8 @@
 
     @pl.when(is_end)
     def _():
+        own_far(1).start()
+        other_far(1).start()
         for k, src in enumerate((far_inner, far_end)):
             for i in range(2):
                 arrived(FR.at[k, i], f_rcv.at[k, i])
@@ -457,12 +451,12 @@
         one = jnp.where(even, pltpu.roll(low, width - refs, 1), high)
         QP[p, c, x] = jnp.where(c == 0, zero, one).astype(jnp.bfloat16)
         QO[p] = jnp.where(c == 0, one, zero).astype(jnp.bfloat16)
-    for k in (2, 0, 1):
-        post_copy(k).start()
-
-    @pl.when(is_end)
-    def _():
-        post_far(c, x).start()
+        for k in (0, 2, 1):
+            post_copy(k, p).start()
+
+        @pl.when(is_end)
+        def _():
+            post_far(c, x, p).start()
 
     for h in halves:
         proj_x(h).wait_send()
@@ -503,12 +497,14 @@
         return carry
 
     lax.fori_loop(0, 4, sent, 0)
-    for i, j in ((1 - c, x), (c, 1 - x), (1 - c, 1 - x)):
-        arrived(QP.at[:, i, j], q_rcv.at[i, j])
+    others = ((1 - c, x, 0), (1 - c, x, 1))
+    others += tuple((i, 1 - x, p) for p in halves for i in (c, 1 - c))
+    for i, j, p in others:
+        arrived(QP.at[p, i, j], q_rcv.at[i, j, p])
 
         @pl.when(is_end)
         def _():
-            post_far(i, j).start()
+            post_far(i, j, p).start()
 
     def turned(block):
         flat = block.reshape(4 * rows, width).astype(jnp.float32)
@@ -573,10 +569,10 @@
             far_core(i).start()
         for i in range(2):
             arrived(XF.at[1 - c, i], xf_rcv.at[1 - c, i, 0])
-        for i in range(2):
-            for j in range(2):
-                arrived(QF.at[:, i, j], qf_rcv.at[i, j])
         for p in halves:
+            for i in range(2):
+                for j in range(2):
+                    arrived(QF.at[p, i, j], qf_rcv.at[i, j, p])
             QTF[p] = turned(QF[p])
 
         def outward(k, d, t):
@@ -635,7 +631,8 @@
         lax.fori_loop(0, T + 4, turn, 0)
 
     for k in range(3):
-        post_copy(k).wait_send()
+        for p in halves:
+            post_copy(k, p).wait_send()
 
     @pl.when(is_end)
     def _():
@@ -644,7 +641,8 @@
             other_far(h).wait_send()
         for i in range(2):
             for j in range(2):
-                post_far(i, j).wait_send()
+                for p in halves:
+                    post_far(i, j, p).wait_send()
 
         def gone(t, carry):
             for k in range(3):
@@ -734,7 +732,7 @@
             pltpu.VMEM((T,) + piece, bf16),
             dma((4,)), dma((2,)), dma((4, 4, 2)), dma((4, 4, 2)), dma((4, 4, 2)), dma((4, 4, 2)),
             dma((2,)), dma((2,)), dma((2, 2, 2)), dma((2, 2)), dma((2,)), dma((2, 2, 2)),
-            dma((4,)), dma((4,)), dma((2, 2)), dma((2, 2)), dma((3,)), dma((2, 2)), dma((2, 2)), dma((2, 2)),
+            dma((4,)), dma((4,)), dma((2, 2)), dma((2, 2)), dma((3, 2)), dma((2, 2, 2)), dma((2, 2, 2)), dma((2, 2, 2)),
             dma((3, TN)), dma((3, TN)), dma((2, T)), dma((2, T)), dma((T,)), dma((T,)),
             dma((T,)), dma((T,)), dma((T,)),
         ],
@@ -745,7 +743,7 @@
             flops=4 * 4 * rows * 4 * width * H // 2, bytes_accessed=4 * rows * coef, transcendentals=0
         ),
     )(images, routes.T, projections[0], noise_weights)
-    block = 2048 if coef % 2048 == 0 else coef
+    block = coef // 2
     sums, norm = pl.pallas_call(
         hand_out,
         grid=(coef // block,),

time: 83.4 us -> 79 us (0.947)
  Pallas kernels: 82.6 us -> 78.3 us
    pallas_call x1, Pallas kernels: 79.3 us -> 76.3 us  [paired_halves(): pl.pallas_call(paired, out_shape=(jax.ShapeDtypeStruct((refs, coef), bf16...]
    pallas_call x1, Pallas kernels: 3.28 us -> 1.97 us  [paired_halves(): pl.pallas_call(hand_out, grid=(coef // block,), out_shape=(jax.ShapeDtype...]
where the time goes in v3:
time: 79 us; the launch traced here: 78.9 us
  Pallas kernels  78.3 us (99%)
    pallas_call x1, Pallas kernels, paired_halves(): pl.pallas_call(paired, out_shape=(jax.ShapeDtypeStruct((refs, coef), bf16...  76.3 us
    pallas_call x1, Pallas kernels, paired_halves(): pl.pallas_call(hand_out, grid=(coef // block,), out_shape=(jax.ShapeDtype...  1.97 us

profile of v3, /device:TPU:0, one launch (start us, length us, event | category | flops | bytes accessed | tf_op | source)
XLA Modules:
  0.0 78.9 jit_solution(15967206835517002624)
XLA Ops:
  0.6 76.3 %shard_map.59 = (bf16[32,8192]{1,0:T(8,128)(2,1)}, f32[1,96]{1,0:T(1,128)}) custom-call(bf16[96,8192]{1,0:T(8,128)(2,1)} %images.1, s32[2,96]{1,0:T(2,128)} %bitcast.6, bf16[32,8192]{1,0:T(8,128)(2,1)} %bitcast.5, f32[8192]{0:T(1024)} %noise_in.1), custom_call_target="tpu_custom_call" | custom-call | flops 1610612736 | bytes 3145728 | tf_op jit(solution)/shard_map/pallas_call | solution.py:699
  76.9 2.0 %shard_map.60 = (f32[32,8192]{1,0:T(8,128)}, f32[1,96]{1,0:T(1,128)}) custom-call(bf16[32,8192]{1,0:T(8,128)(2,1)} %get-tuple-element.6.sums_in, f32[1,96]{1,0:T(1,128)} %get-tuple-element.7.norm_in), custom_call_target="tpu_custom_call" | custom-call | tf_op jit(solution)/shard_map/pallas_call | solution.py:747

commit v4 on v3

v4 whole, which is shorter than its diff:
```python
from functools import partial

import jax
import jax.numpy as jnp
from jax import lax
from jax.experimental import pallas as pl
from jax.experimental.pallas import tpu as pltpu
from jax.sharding import PartitionSpec as P

MESH = pl.DeviceIdType.MESH


def from_behind(block, axis, distance):
    devices = range(lax.axis_size(axis))
    route = [((i - distance) % len(devices), i) for i in devices]
    return lax.ppermute(block, axis, route)


def slot_positions(route_block):
    flat = route_block.reshape(-1)
    order = jnp.arange(flat.shape[0], dtype=jnp.int32)
    earlier = (order[None, :] < order[:, None]) & (flat[None, :] == flat[:, None])
    return jnp.sum(earlier.astype(jnp.int32), axis=1).reshape(route_block.shape)


def combine_stats(row_peaks, row_totals):
    highest = jnp.max(row_peaks, axis=-1)
    spread = row_totals * jnp.exp(row_peaks - highest[..., None])
    return highest + jnp.log(jnp.sum(spread, axis=-1))


def routed(images, routes, projections, noise_weights):
    groups = lax.axis_size("reader")
    cycle_size = lax.axis_size("blk")
    my_group = lax.axis_index("reader")
    my_member = lax.axis_index("blk")
    per_device, top_count = routes.shape
    half_width = images.shape[1]
    capacity = min(per_device, 2 * per_device * top_count // groups)
    slot_count = groups * capacity
    ref_count = projections.shape[1]
    all_refs = ref_count * cycle_size
    anchor = jnp.zeros((), jnp.int32)
    own_index = slot_positions(routes)
    own_target = routes * capacity + own_index
    sources = jnp.broadcast_to(jnp.arange(per_device, dtype=jnp.int32)[:, None], routes.shape)
    picker = (
        jnp.full((slot_count,), per_device, jnp.int32)
        .at[own_target.reshape(-1)]
        .set(sources.reshape(-1))
    )
    padded = jnp.concatenate([images, jnp.zeros((1, half_width), images.dtype)], axis=0)
    outgoing = padded[picker].reshape(groups, capacity, half_width)
    received = lax.all_to_all(outgoing, "reader", split_axis=0, concat_axis=0, tiled=True).reshape(
        slot_count, half_width
    )
    every_route = lax.all_gather(routes, "reader", axis=0, tiled=True).reshape(
        groups, per_device, top_count
    )
    every_index = jax.vmap(slot_positions)(every_route)
    senders = jnp.arange(groups, dtype=jnp.int32)[:, None, None]
    landing = jnp.where(every_route == my_group, senders * capacity + every_index, slot_count)
    live_slot = jnp.zeros((slot_count,), jnp.int32).at[landing.reshape(-1)].set(1, mode="drop") > 0

    def score_block(ref_block):
        scaled = ref_block.astype(jnp.float32) * noise_weights[None, :]
        weighted = scaled.astype(jnp.bfloat16)
        penalty = 0.5 * jnp.sum(scaled * ref_block.astype(jnp.float32), axis=1)
        partial_scores = lax.dot_general(
            weighted, received, (((1,), (1,)), ((), ())), preferred_element_type=jnp.float32
        )
        return partial_scores - penalty[:, None]

    def cycle_turn(rotation, carry):
        ref_block, score_table = carry
        position = (my_member - rotation) % cycle_size
        score_table = lax.dynamic_update_slice(
            score_table, score_block(ref_block)[None], (position, anchor, anchor)
        )
        ref_block = from_behind(ref_block, "blk", 1)
        return (ref_block, score_table)

    empty_table = jnp.zeros((cycle_size, ref_count, slot_count), jnp.float32)
    ref_block, score_table = lax.fori_loop(
        0, cycle_size - 1, cycle_turn, (projections[0], empty_table)
    )
    position = (my_member + 1) % cycle_size
    score_table = lax.dynamic_update_slice(
        score_table, score_block(ref_block)[None], (position, anchor, anchor)
    )
    score_table = lax.psum(score_table, "sub")
    scores = score_table.reshape(all_refs, slot_count)
    row_peak = jnp.max(scores, axis=0)
    row_total = jnp.sum(jnp.exp(scores - row_peak[None, :]), axis=0)
    back_peak, back_total = (
        lax.all_to_all(
            row_peak.reshape(groups, capacity), "reader", split_axis=0, concat_axis=0, tiled=True
        ),
        lax.all_to_all(
            row_total.reshape(groups, capacity), "reader", split_axis=0, concat_axis=0, tiled=True
        ),
    )
    normalizer = combine_stats(
        back_peak.reshape(-1)[own_target], back_total.reshape(-1)[own_target]
    )
    outgoing_norm = (
        jnp.zeros((slot_count,), jnp.float32)
        .at[own_target.reshape(-1)]
        .set(jnp.repeat(normalizer, top_count))
    )
    slot_norm = lax.all_to_all(
        outgoing_norm.reshape(groups, capacity), "reader", split_axis=0, concat_axis=0, tiled=True
    ).reshape(slot_count)
    exponent = jnp.where(live_slot[None, :], scores - slot_norm[None, :], -jnp.inf)
    posterior = jnp.exp(exponent).astype(jnp.bfloat16)
    summed = lax.psum_scatter(
        jnp.dot(posterior, received, preferred_element_type=jnp.float32).astype(jnp.bfloat16),
        "blk",
        scatter_dimension=0,
        tiled=True,
    ).astype(jnp.float32)
    return (summed[None], normalizer)


LOW = 3
CUTS = (3, 5, 8)


def paired(
    images, routes_in, proj, noise_in,
    out, norm,
    routes, noise, X, XF, PR, S, SC, SR, MOVE, SAME, SF, FR, QP, QO, QF, QT, QTF, PROD, TE, RE, TM, RM, TI, RI, O,
    loc, rt_snd, rt_rcv, px_snd, pb_snd, pm_snd, pc_snd, p_rcv, c_rcv, xx_snd, xc_snd, x_rcv, xf_snd, xfc_snd, xf_rcv,
    s_snd, s_rcv, f_snd, f_rcv, q_snd, q_rcv, qf_snd, qf_rcv, e_snd, e_rcv, m_snd, m_rcv, i_snd, i_rcv,
    own_snd, o_snd, o_rcv,
):
    r = lax.axis_index("reader")
    b = lax.axis_index("blk")
    x, c = r // 2, r % 2
    rx, rc = (r + 2) % 4, x * 2 + 1 - c
    rd = (rc + 2) % 4
    side = b // 2
    inner, end = 1 + side, 3 * side
    far_inner, far_end = 2 - side, 3 - 3 * side
    buddy, across = inner + end - b, 3 - b
    is_end = b == end
    is_inner = b == inner
    rows = images.shape[0]
    refs = proj.shape[0]
    H = X.shape[4 - 1]
    F = H // 2
    T, tile = O.shape[0], O.shape[3]
    TF = F // tile
    low = LOW * tile
    width = 4 * refs
    halves = (0, 1)
    pairs = (1 - side, side)
    marks = (0,) + CUTS
    whole = tuple((a * tile, (e - a) * tile) for a, e in zip(marks, CUTS))
    bits = range(len(CUTS))
    late = bits[1:]
    queue = tuple(late) + (0,)
    strips = ((0, low), (low, H - low))
    far_strips = ((0, low), (low, F - low))

    def remote(src, dst, snd, rcv, **where):
        return pltpu.make_async_remote_copy(
            src_ref=src, dst_ref=dst, send_sem=snd, recv_sem=rcv,
            device_id=where, device_id_type=MESH,
        )

    def arrived(dst, sem):
        remote(dst, dst, sem, sem, reader=rx).wait_recv()

    def left(src, sem):
        remote(src, src, sem, sem, reader=rx).wait_send()

    def columns(i, cut):
        return pl.ds(pl.multiple_of(i * H + cut[0], tile), cut[1])

    def part(src, g, cut):
        return PR.at[src, g, :, pl.ds(*cut)]

    def own_piece(h):
        return proj.at[:, columns(x, whole[h])]

    def proj_x(h):
        return remote(
            proj.at[:, columns(1 - x, whole[h])], part(b, r, whole[h]), px_snd.at[0], p_rcv.at[b, x, h], reader=rx
        )

    def stage(h):
        return h // (len(CUTS) - 1)

    def to_core(piece, src, g, h):
        late_one = is_end & (src != b) & (src != buddy)
        return remote(
            piece, part(src, g, whole[h]), pc_snd.at[late_one.astype(jnp.int32)], c_rcv.at[src, stage(h)], reader=rc
        )

    def to_buddy(piece, src, g, h):
        return remote(
            piece, part(src, g, whole[h]), pb_snd.at[(src != b).astype(jnp.int32)], p_rcv.at[src, g // 2, h], blk=buddy
        )

    def to_across(piece, src, g, h):
        return remote(piece, part(src, g, whole[h]), pm_snd.at[0], p_rcv.at[src, g // 2, h], blk=across)

    def image_x(h):
        return remote(
            images.at[:, columns(1 - x, strips[h])], X.at[c, x, :, pl.ds(*strips[h])],
            xx_snd.at[0], x_rcv.at[h], reader=rx,
        )

    def own_image_core():
        return remote(
            images.at[:, pl.ds(pl.multiple_of(x * H, H), H)], X.at[c, x],
            xc_snd.at[0], x_rcv.at[2], reader=rc,
        )

    def other_image_core():
        return remote(X.at[c, 1 - x], X.at[c, 1 - x], xc_snd.at[0], x_rcv.at[2], reader=rc)

    def own_far(h):
        return remote(
            images.at[:, columns(x, far_strips[h])], XF.at[c, x, :, pl.ds(*far_strips[h])],
            xf_snd.at[0], xf_rcv.at[h], blk=buddy,
        )

    def other_far(h):
        return remote(
            X.at[c, 1 - x, :, pl.ds(*far_strips[h])], XF.at[c, 1 - x, :, pl.ds(*far_strips[h])],
            xf_snd.at[0], xf_rcv.at[h], blk=buddy,
        )

    def far_core(i):
        return remote(XF.at[c, i], XF.at[c, i], xfc_snd.at[0], xf_rcv.at[2], reader=rc)

    def score_copy(q):
        return remote(SC.at[q], SR.at[q], s_snd.at[0], s_rcv.at[q], reader=rx)

    def routes_x():
        return remote(routes_in, routes.at[x], rt_snd.at[0], rt_rcv.at[0], reader=rx)

    def far_score(k, i):
        if i == 0:
            return remote(SF.at[k, x], FR.at[k, x], f_snd.at[0], f_rcv.at[0], blk=buddy)
        return remote(SF.at[k, 1 - x], FR.at[k, x], f_snd.at[0], f_rcv.at[0], blk=buddy, reader=rx)

    def post_copy(k, p):
        source, to = ((QP.at[p, c, x], rx), (QO.at[p], rc), (QO.at[p], rd))[k]
        return remote(source, QP.at[p, c, x], q_snd.at[k % 2], q_rcv.at[c, x, p], reader=to)

    def post_far(i, j, p):
        return remote(QP.at[p, i, j], QF.at[p, i, j], qf_snd.at[0], qf_rcv.at[p], blk=buddy)

    def end_copy(k, t):
        return remote(TE.at[k, t], RE.at[k, t], e_snd.at[0], e_rcv.at[k, t], blk=buddy)

    def middle_copy(k, t):
        return remote(TM.at[k, t], RM.at[k, t], m_snd.at[0], m_rcv.at[k, t], blk=across)

    def inner_copy(t):
        return remote(TI.at[t], RI.at[t], i_snd.at[0], i_rcv.at[t], blk=buddy)

    def out_span(i, t):
        return out.at[:, pl.ds(pl.multiple_of(i * H + t * tile, tile), tile)]

    def out_x(src, t):
        return remote(src.at[t, 1 - x], out_span(x, t), o_snd.at[0], o_rcv.at[0], reader=rx)

    def out_own(src, t):
        return pltpu.make_async_copy(src.at[t, x], out_span(x, t), own_snd.at[0])

    own_proj = pltpu.make_async_copy(proj.at[:, pl.ds(pl.multiple_of(x * H, H), H)], PR.at[b, r], loc.at[0])
    own_image = pltpu.make_async_copy(
        images.at[:, pl.ds(pl.multiple_of(x * H, H), H)], X.at[c, x], loc.at[1]
    )
    noise_copy = pltpu.make_async_copy(
        noise_in.at[pl.ds(pl.multiple_of(x * H, H), H)], noise, loc.at[2]
    )
    routes_copy = pltpu.make_async_copy(routes_in, routes.at[x], loc.at[3])

    barrier = pltpu.get_barrier_semaphore()
    for k in (rx, rc, rd):
        pl.semaphore_signal(barrier, inc=1, device_id={"reader": k}, device_id_type=MESH)
    pl.semaphore_signal(barrier, inc=1, device_id={"blk": buddy}, device_id_type=MESH)
    pl.semaphore_signal(barrier, inc=1, device_id={"blk": buddy, "reader": rx}, device_id_type=MESH)

    @pl.when(is_inner)
    def _():
        pl.semaphore_signal(barrier, inc=1, device_id={"blk": across}, device_id_type=MESH)

    own_proj.start()
    own_image.start()
    noise_copy.start()
    routes_copy.start()
    pl.semaphore_wait(barrier, 5 + is_inner.astype(jnp.int32))

    def spread(piece, g, h):
        to_buddy(piece, b, g, h).start()

        @pl.when(is_inner)
        def _():
            to_across(piece, b, g, h).start()

    routes_x().start()
    for h in queue:
        proj_x(h).start()
        if h > 0:
            spread(own_piece(h), r, h)
    for h in queue:
        to_core(own_piece(h), b, r, h).start()
    for h in queue:
        piece = part(b, rx, whole[h])
        arrived(piece, p_rcv.at[b, 1 - x, h])
        if h == 0:
            spread(own_piece(h), r, h)
        spread(piece, rx, h)
        to_core(piece, b, rx, h).start()
        if h == queue[1]:
            for k in halves:
                image_x(k).start()
    own_image_core().start()

    late_pieces = tuple((g, h) for g in (r, rx) for h in late)
    pieces = late_pieces + ((r, 0), (rx, 0))

    def other_image(h):
        arrived(X.at[c, 1 - x, :, pl.ds(*strips[h])], x_rcv.at[h])

    def hand_over(src, g, h):
        piece = part(src, g, whole[h])
        arrived(piece, p_rcv.at[src, g // 2, h])
        to_core(piece, src, g, h).start()

    @pl.when(is_end)
    def _():
        for g, h in pieces[:4]:
            hand_over(buddy, g, h)
        own_far(0).start()
        for g, h in pieces[4:]:
            hand_over(buddy, g, h)
        other_image(0)
        other_far(0).start()
        for g, h in late_pieces:
            hand_over(far_inner, g, h)
        other_image(1)
        own_far(1).start()
        other_far(1).start()
        for g, h in late_pieces[:-2]:
            hand_over(far_end, g, h)

    @pl.when(is_inner)
    def _():
        for g, h in pieces:
            arrived(part(far_inner, g, whole[h]), p_rcv.at[far_inner, g // 2, h])
            if h > 0:
                to_buddy(part(far_inner, g, whole[h]), far_inner, g, h).start()
            to_core(part(far_inner, g, whole[h]), far_inner, g, h).start()
            arrived(part(buddy, g, whole[h]), p_rcv.at[buddy, g // 2, h])
            to_across(part(buddy, g, whole[h]), buddy, g, h).start()
            to_core(part(buddy, g, whole[h]), buddy, g, h).start()
        for g, h in pieces:
            arrived(part(far_end, g, whole[h]), p_rcv.at[far_end, g // 2, h])
            if h > 0:
                to_buddy(part(far_end, g, whole[h]), far_end, g, h).start()
            to_core(part(far_end, g, whole[h]), far_end, g, h).start()
        for h in halves:
            other_image(h)

    other_image_core().start()
    own_proj.wait()
    own_image.wait()
    noise_copy.wait()
    routes_copy.wait()

    arrived(routes.at[1 - x], rt_rcv.at[0])
    lane = lax.broadcasted_iota(jnp.int32, (rows, width), 1)
    block = lane // refs
    diagonal = lax.broadcasted_iota(jnp.int32, (rows, rows), 0) == lax.broadcasted_iota(
        jnp.int32, (rows, rows), 1
    )

    def column(row):
        return jnp.sum(jnp.where(diagonal, row, 0.0), axis=1, keepdims=True).astype(jnp.int32)

    for i in range(2):
        names = routes[i].astype(jnp.float32)
        first, second = column(names[0:1]), column(names[1:2])
        MOVE[i] = (block - jnp.where(block < 2, first, second) + 4) % 4
        @pl.when(i == x)
        def _():
            SAME[0] = jnp.where(block < 2, first, second)
            SAME[1] = jnp.where(block < 2, second, first)

    def packed(p, i):
        even = block % 2 == 0
        low, high, move = S[2 * p, i], S[2 * p + 1, i], MOVE[i]
        total = jnp.where(even, low, high)
        for m in range(1, 4):
            turned_by = jnp.where(even, pltpu.roll(low, m * refs, 1), pltpu.roll(high, m * refs, 1))
            total = jnp.where(move == m, turned_by, total)
        return total

    square = lax.broadcasted_iota(jnp.int32, (width, width), 0) == lax.broadcasted_iota(
        jnp.int32, (width, width), 1
    )

    def scores_of(block, src, tiles):
        scores = jnp.zeros((2 * rows, width), jnp.float32)
        penalty = jnp.zeros((width, 128), jnp.float32)
        for t in tiles:
            cut = pl.ds(t * tile, tile)
            refs_f = PR[src, :, :, cut].reshape(width, tile).astype(jnp.float32)
            scaled = refs_f * noise[cut][None, :]
            scores = scores + lax.dot_general(
                block[c, :, :, cut].reshape(2 * rows, tile), scaled.astype(jnp.bfloat16),
                (((1,), (1,)), ((), ())), preferred_element_type=jnp.float32,
            )
            squares = scaled * refs_f
            for lane in range(0, tile, 128):
                penalty = penalty + squares[:, lane : lane + 128]
        lanes = jnp.sum(penalty, axis=1, keepdims=True)
        penalty_row = 0.5 * jnp.sum(jnp.where(square, lanes, 0.0), axis=0, keepdims=True)
        return (scores - penalty_row).reshape(2, rows, width)

    def from_core(src, n, first):
        start = marks[first]
        both = PR.at[src, pl.ds(0, 2), :, pl.ds(start * tile, (CUTS[-2 + n] - start) * tile)]
        arrived(both, c_rcv.at[src, n])

    @pl.when(is_inner)
    def _():
        arrived(XF.at[c, :, :, pl.ds(*far_strips[0])], xf_rcv.at[0])

        def far_source(k, carry):
            src = jnp.where(k == 0, far_inner, far_end)
            from_core(src, 0, 0)
            from_core(src, 1, len(CUTS) - 1)
            SF[k] = scores_of(XF, src, range(LOW))
            for i in (1, 0):
                far_score(k, i).start()
            return carry

        lax.fori_loop(0, 2, far_source, 0)

    def score_source(i, carry):
        src = jnp.where(i == 0, b, jnp.where(i == 1, buddy, jnp.where(i == 2, far_inner, far_end)))

        @pl.when(i < 2)
        def _():
            from_core(src, 0, 0)
            from_core(src, 1, len(CUTS) - 1)

        @pl.when((i < 2) | is_inner)
        def _():
            S[src] = scores_of(X, src, range(T))

        @pl.when((i >= 2) & is_end)
        def _():
            @pl.when(i == 3)
            def _():
                hand_over(src, *late_pieces[-2])

            from_core(src, 0, 1)
            S[src] = scores_of(X, src, range(LOW, CUTS[-2]))

            @pl.when(i == 3)
            def _():
                hand_over(src, *late_pieces[-1])

            from_core(src, 1, len(CUTS) - 1)
            S[src] = S[src] + scores_of(X, src, range(CUTS[-2], T))

        @pl.when(i % 2 == 1)
        def _():
            q = i // 2
            SC[q] = packed(side + q * (1 - 2 * side), 1 - x)
            score_copy(q).start()

        return carry

    lax.fori_loop(0, 4, score_source, 0)

    @pl.when(is_end)
    def _():
        arrived(FR, f_rcv.at[0])
        for k, src in enumerate((far_inner, far_end)):
            S[src, x] = S[src, x] + FR[k, 0] + FR[k, 1]

    chunks = []
    for q, p in enumerate(pairs):
        arrived(SR.at[1 - q], s_rcv.at[1 - q])
        chunks.append(packed(p, x) + SR[1 - q])
    highest = jnp.max(jnp.maximum(chunks[0], chunks[1]), axis=1, keepdims=True)
    total = jnp.exp(chunks[0] - highest) + jnp.exp(chunks[1] - highest)
    normalizer = highest + jnp.log(jnp.sum(total, axis=1, keepdims=True))
    norm[...] = jnp.sum(jnp.where(diagonal, normalizer, 0.0), axis=0, keepdims=True)

    def for_core(value, core):
        group = core + 2 * (lane // (2 * refs))
        swapped = jnp.where(SAME[1] == group, pltpu.roll(value, 2 * refs, 1), 0.0)
        return jnp.where(SAME[0] == group, value, swapped).astype(jnp.bfloat16)

    for q, p in enumerate(pairs):
        value = jnp.exp(chunks[q] - normalizer)
        QP[p, c, x] = for_core(value, c)
        QO[p] = for_core(value, 1 - c)
        for k in (0, 2, 1):
            post_copy(k, p).start()

        @pl.when(is_end)
        def _():
            post_far(c, x, p).start()

    for p in pairs:
        for i, j in ((1 - c, x), (c, 1 - x), (1 - c, 1 - x)):
            arrived(QP.at[p, i, j], q_rcv.at[i, j, p])

            @pl.when(is_end)
            def _():
                post_far(i, j, p).start()

    left(PR.at[0, 0], px_snd.at[0])
    left(X.at[0, 0], xx_snd.at[0])
    left(X.at[0], xc_snd.at[0])
    left(SC, s_snd.at[0])
    routes_x().wait_send()
    late_columns = pl.ds(low, H - low)
    left(PR.at[0, pl.ds(0, 2)], pb_snd.at[0])

    @pl.when(is_end)
    def _():
        left(PR.at[pl.ds(0, 2), pl.ds(0, 2)], pc_snd.at[0])
        left(PR.at[pl.ds(0, 2), pl.ds(0, 2), :, late_columns], pc_snd.at[1])

    @pl.when(is_inner)
    def _():
        left(PR.at[:, pl.ds(0, 2)], pc_snd.at[0])
        left(PR.at[pl.ds(0, 2), pl.ds(0, 2), :, late_columns], pb_snd.at[1])
        left(PR.at[pl.ds(0, 2), pl.ds(0, 2)], pm_snd.at[0])

    def turned(block):
        flat = block.reshape(4 * rows, width).astype(jnp.float32)
        return flat.T.astype(jnp.bfloat16)

    for p in halves:
        QT[p] = turned(QP[p])
    arrived(X.at[1 - c], x_rcv.at[2])

    def product(left, right):
        return lax.dot_general(
            left, right.reshape(4 * rows, tile), (((1,), (0,)), ((), ())), preferred_element_type=jnp.float32
        )

    def span(t):
        return pl.ds(pl.multiple_of(t * tile, tile), tile)

    def multiply(q, t, both):
        total = product(QT[pairs[q]], X[:, :, :, span(t)])
        if both:
            total = total + product(QTF[pairs[q]], XF[:, :, :, span(t)])
        PROD[t, q] = total.reshape(2, 2, refs, tile)

    def own(t, q, d):
        return PROD[t, q, :, d % 2]

    def f32(value):
        return value.astype(jnp.float32)

    @pl.when(is_end)
    def _():
        def send(t, carry):
            for k, q, d in ((1, 0, far_end), (0, 0, far_inner), (2, 1, inner)):
                if k != 0:
                    multiply(q, t, False)
                TE[k, t - TF] = own(t, q, d).astype(jnp.bfloat16)
                end_copy(k, t - TF).start()
            return carry

        def pass_on(t, carry):
            arrived(RI.at[t], i_rcv.at[t])
            out_x(RI, t).start()
            out_own(RI, t).start()
            return carry

        def finish(t, carry):
            arrived(RI.at[t], i_rcv.at[t])
            O[t] = (own(t, 1, end) + f32(RI[t])).astype(jnp.bfloat16)
            out_x(O, t).start()
            out_own(O, t).start()
            return carry

        left(QP, qf_snd.at[0])
        lax.fori_loop(TF, T, send, 0)
        lax.fori_loop(0, TF, pass_on, 0)
        lax.fori_loop(TF, T, finish, 0)

    @pl.when(is_inner)
    def _():
        arrived(XF.at[c, :, :, pl.ds(*far_strips[1])], xf_rcv.at[1])
        for i in range(2):
            far_core(i).start()
        arrived(XF.at[1 - c], xf_rcv.at[2])

        def far_posterior(q):
            p = pairs[q]
            arrived(QF.at[p], qf_rcv.at[p])
            QTF[p] = turned(QF[p])

        def multiply_any(q, t):
            @pl.when(t < TF)
            def _():
                multiply(q, t, True)

            @pl.when(t >= TF)
            def _():
                multiply(q, t, False)

        far_posterior(0)

        def outward(k, d, t):
            @pl.when(t < TF)
            def _():
                TM[k, t] = own(t, 0, d).astype(jnp.bfloat16)

            @pl.when(t >= TF)
            def _():
                arrived(RE.at[k, t - TF], e_rcv.at[k, t - TF])
                TM[k, t] = (own(t, 0, d) + f32(RE[k, t - TF])).astype(jnp.bfloat16)

            middle_copy(k, t).start()

        def turn(t, carry):
            @pl.when(t < T)
            def _():
                multiply_any(0, t)
                outward(1, far_end, t)

            @pl.when((t >= 2) & (t < T + 2))
            def _():
                outward(0, far_inner, t - 2)

            @pl.when(t == 1)
            def _():
                far_posterior(1)

            @pl.when((t >= 1) & (t < T + 1))
            def _():
                multiply_any(1, t - 1)

            @pl.when((t >= 2) & (t < T + 2))
            def _():
                n = t - 2
                arrived(RM.at[1, n], m_rcv.at[1, n])
                TI[n] = (own(n, 1, end) + f32(RM[1, n])).astype(jnp.bfloat16)
                inner_copy(n).start()

            @pl.when(t >= 4)
            def _():
                n = t - 4
                arrived(RM.at[0, n], m_rcv.at[0, n])
                total = own(n, 1, inner) + f32(RM[0, n])

                @pl.when(n < TF)
                def _():
                    O[n] = total.astype(jnp.bfloat16)

                @pl.when(n >= TF)
                def _():
                    arrived(RE.at[2, n - TF], e_rcv.at[2, n - TF])
                    O[n] = (total + f32(RE[2, n - TF])).astype(jnp.bfloat16)

                out_x(O, n).start()
                out_own(O, n).start()

            return carry

        lax.fori_loop(0, T + 4, turn, 0)

    left(QP.at[0], q_snd.at[0])
    left(QP.at[0, 0], q_snd.at[1])

    @pl.when(is_end)
    def _():
        left(XF.at[0], xf_snd.at[0])
        left(TE, e_snd.at[0])

    @pl.when(is_inner)
    def _():
        left(XF.at[0], xfc_snd.at[0])
        left(SF, f_snd.at[0])
        left(TM, m_snd.at[0])
        left(TI, i_snd.at[0])

    left(O.at[:, 0], o_snd.at[0])
    pltpu.make_async_copy(O.at[:, 0], O.at[:, 0], own_snd.at[0]).wait()
    arrived(out.at[:, pl.ds(pl.multiple_of((1 - x) * H, H), H)], o_rcv.at[0])


def hand_out(sums_in, norm_in, sums_out, norm_out):
    sums_out[...] = sums_in[...].astype(jnp.float32)
    norm_out[...] = norm_in[...]


def paired_halves(images, routes, projections, noise_weights):
    rows, coef = images.shape
    refs = projections.shape[1]
    H, width = coef // 2, 4 * refs
    F = H // 2
    T, TF = 8, 4
    tile = H // T
    TN = T - TF
    dma = pltpu.SemaphoreType.DMA
    bf16, f32 = jnp.bfloat16, jnp.float32
    piece = (2, refs, tile)
    sums, norm = pl.pallas_call(
        paired,
        out_shape=(
            jax.ShapeDtypeStruct((refs, coef), bf16),
            jax.ShapeDtypeStruct((1, rows), f32),
        ),
        in_specs=[pl.BlockSpec(memory_space=pltpu.HBM)] * 4,
        out_specs=(
            pl.BlockSpec(memory_space=pl.ANY),
            pl.BlockSpec(memory_space=pltpu.VMEM),
        ),
        scratch_shapes=[
            pltpu.VMEM((2, 2, rows), jnp.int32),
            pltpu.VMEM((H,), f32),
            pltpu.VMEM((2, 2, rows, H), bf16),
            pltpu.VMEM((2, 2, rows, F), bf16),
            pltpu.VMEM((4, 4, refs, H), bf16),
            pltpu.VMEM((4, 2, rows, width), f32),
            pltpu.VMEM((2, rows, width), f32),
            pltpu.VMEM((2, rows, width), f32),
            pltpu.VMEM((2, rows, width), jnp.int32),
            pltpu.VMEM((2, rows, width), jnp.int32),
            pltpu.VMEM((2, 2, rows, width), f32),
            pltpu.VMEM((2, 2, rows, width), f32),
            pltpu.VMEM((2, 2, 2, rows, width), bf16),
            pltpu.VMEM((2, rows, width), bf16),
            pltpu.VMEM((2, 2, 2, rows, width), bf16),
            pltpu.VMEM((2, width, 4 * rows), bf16),
            pltpu.VMEM((2, width, 4 * rows), bf16),
            pltpu.VMEM((T, 2, 2, 2, refs, tile), f32),
            pltpu.VMEM((3, TN) + piece, bf16),
            pltpu.VMEM((3, TN) + piece, bf16),
            pltpu.VMEM((2, T) + piece, bf16),
            pltpu.VMEM((2, T) + piece, bf16),
            pltpu.VMEM((T,) + piece, bf16),
            pltpu.VMEM((T,) + piece, bf16),
            pltpu.VMEM((T,) + piece, bf16),
            dma((4,)), dma((1,)), dma((1,)), dma((1,)), dma((2,)), dma((1,)), dma((2,)),
            dma((4, 2, len(CUTS))), dma((4, 2)), dma((1,)), dma((1,)), dma((3,)), dma((1,)), dma((1,)), dma((3,)),
            dma((1,)), dma((2,)), dma((1,)), dma((1,)), dma((2,)), dma((2, 2, 2)), dma((1,)), dma((2,)),
            dma((1,)), dma((3, TN)), dma((1,)), dma((2, T)), dma((1,)), dma((T,)),
            dma((1,)), dma((1,)), dma((1,)),
        ],
        compiler_params=pltpu.CompilerParams(
            collective_id=0, has_side_effects=True, vmem_limit_bytes=64 * 1024 * 1024 - 65536
        ),
        cost_estimate=pl.CostEstimate(
            flops=4 * 4 * rows * 4 * width * H // 2, bytes_accessed=4 * rows * coef, transcendentals=0
        ),
    )(images, routes.T, projections[0], noise_weights)
    block = coef // 2
    sums, norm = pl.pallas_call(
        hand_out,
        grid=(coef // block,),
        out_shape=(jax.ShapeDtypeStruct((refs, coef), f32), jax.ShapeDtypeStruct((1, rows), f32)),
        in_specs=[pl.BlockSpec((refs, block), lambda i: (0, i)), pl.BlockSpec((1, rows), lambda i: (0, 0))],
        out_specs=(pl.BlockSpec((refs, block), lambda i: (0, i)), pl.BlockSpec((1, rows), lambda i: (0, 0))),
    )(sums, norm)
    return (sums[None], norm[0])


def solution(mesh):
    sizes = dict(mesh.shape)
    direct = sizes["sub"] == 1 and sizes["reader"] == 4 and sizes["blk"] == 4
    return jax.shard_map(
        paired_halves if direct else routed,
        mesh=mesh,
        in_specs=(
            P(("parts", "blk", "reader"), "sub"),
            P(("parts", "blk", "reader"), None),
            P(("parts", "reader"), "blk", "sub"),
            P(("parts", "sub")),
        ),
        out_specs=(P(("parts", "reader"), "blk", "sub"), P(("parts", "blk", "reader"))),
        check_vma=False,
    )
```

time: 79 us -> 78.5 us (level)
  no operation moved by 1% of the time
where the time goes in v4:
time: 78.5 us; the launch traced here: 78.3 us
  Pallas kernels  77.7 us (99%)
    pallas_call x1, Pallas kernels, paired_halves(): pl.pallas_call(paired, out_shape=(jax.ShapeDtypeStruct((refs, coef), bf16...  75.7 us
    pallas_call x1, Pallas kernels, paired_halves(): pl.pallas_call(hand_out, grid=(coef // block,), out_shape=(jax.ShapeDtype...  1.97 us

profile of v4, /device:TPU:0, one launch (start us, length us, event | category | flops | bytes accessed | tf_op | source)
XLA Modules:
  0.0 78.3 jit_solution(18055477715007543180)
XLA Ops:
  0.6 75.7 %shard_map.59 = (bf16[32,8192]{1,0:T(8,128)(2,1)}, f32[1,96]{1,0:T(1,128)}) custom-call(bf16[96,8192]{1,0:T(8,128)(2,1)} %images.1, s32[2,96]{1,0:T(2,128)} %bitcast.6, bf16[32,8192]{1,0:T(8,128)(2,1)} %bitcast.5, f32[8192]{0:T(1024)} %noise_in.1), custom_call_target="tpu_custom_call" | custom-call | flops 1610612736 | bytes 3145728 | tf_op jit(solution)/shard_map/pallas_call | solution.py:718
  76.3 2.0 %shard_map.60 = (f32[32,8192]{1,0:T(8,128)}, f32[1,96]{1,0:T(1,128)}) custom-call(bf16[32,8192]{1,0:T(8,128)(2,1)} %get-tuple-element.6.sums_in, f32[1,96]{1,0:T(1,128)} %get-tuple-element.7.norm_in), custom_call_target="tpu_custom_call" | custom-call | tf_op jit(solution)/shard_map/pallas_call | solution.py:769

commit v5 on v4

--- a/solution.py
+++ b/solution.py
@@ -123,7 +123,7 @@
 
 
 LOW = 3
-CUTS = (3, 5, 8)
+CUTS = (3, 6, 8)
 
 
 def paired(
@@ -159,7 +159,6 @@
     whole = tuple((a * tile, (e - a) * tile) for a, e in zip(marks, CUTS))
     bits = range(len(CUTS))
     late = bits[1:]
-    queue = tuple(late) + (0,)
     strips = ((0, low), (low, H - low))
     far_strips = ((0, low), (low, F - low))
 
@@ -305,26 +304,23 @@
             to_across(piece, b, g, h).start()
 
     routes_x().start()
-    for h in queue:
+    for h in bits:
         proj_x(h).start()
-        if h > 0:
-            spread(own_piece(h), r, h)
-    for h in queue:
+        spread(own_piece(h), r, h)
+    for h in bits:
         to_core(own_piece(h), b, r, h).start()
-    for h in queue:
+    for h in bits:
         piece = part(b, rx, whole[h])
         arrived(piece, p_rcv.at[b, 1 - x, h])
-        if h == 0:
-            spread(own_piece(h), r, h)
         spread(piece, rx, h)
         to_core(piece, b, rx, h).start()
-        if h == queue[1]:
+        if h == 0:
             for k in halves:
                 image_x(k).start()
     own_image_core().start()
 
     late_pieces = tuple((g, h) for g in (r, rx) for h in late)
-    pieces = late_pieces + ((r, 0), (rx, 0))
+    pieces = tuple((g, h) for g in (r, rx) for h in bits)
 
     def other_image(h):
         arrived(X.at[c, 1 - x, :, pl.ds(*strips[h])], x_rcv.at[h])
@@ -346,8 +342,6 @@
         for g, h in late_pieces:
             hand_over(far_inner, g, h)
         other_image(1)
-        own_far(1).start()
-        other_far(1).start()
         for g, h in late_pieces[:-2]:
             hand_over(far_end, g, h)
 
@@ -485,6 +479,8 @@
 
     @pl.when(is_end)
     def _():
+        own_far(1).start()
+        other_far(1).start()
         arrived(FR, f_rcv.at[0])
         for k, src in enumerate((far_inner, far_end)):
             S[src, x] = S[src, x] + FR[k, 0] + FR[k, 1]

time: 78.5 us -> 76.8 us (0.978)
  Pallas kernels: 77.7 us -> 76.1 us
    pallas_call x1, Pallas kernels: 75.7 us -> 74.1 us  [paired_halves(): pl.pallas_call(paired, out_shape=(jax.ShapeDtypeStruct((refs, coef), bf16...]
where the time goes in v5:
time: 76.8 us; the launch traced here: 76.7 us
  Pallas kernels  76.1 us (99%)
    pallas_call x1, Pallas kernels, paired_halves(): pl.pallas_call(paired, out_shape=(jax.ShapeDtypeStruct((refs, coef), bf16...  74.1 us
    pallas_call x1, Pallas kernels, paired_halves(): pl.pallas_call(hand_out, grid=(coef // block,), out_shape=(jax.ShapeDtype...  1.97 us

profile of v5, /device:TPU:0, one launch (start us, length us, event | category | flops | bytes accessed | tf_op | source)
XLA Modules:
  0.0 76.7 jit_solution(5381279030840562436)
XLA Ops:
  0.6 74.1 %shard_map.59 = (bf16[32,8192]{1,0:T(8,128)(2,1)}, f32[1,96]{1,0:T(1,128)}) custom-call(bf16[96,8192]{1,0:T(8,128)(2,1)} %images.1, s32[2,96]{1,0:T(2,128)} %bitcast.6, bf16[32,8192]{1,0:T(8,128)(2,1)} %bitcast.5, f32[8192]{0:T(1024)} %noise_in.1), custom_call_target="tpu_custom_call" | custom-call | flops 1610612736 | bytes 3145728 | tf_op jit(solution)/shard_map/pallas_call | solution.py:714
  74.7 2.0 %shard_map.60 = (f32[32,8192]{1,0:T(8,128)}, f32[1,96]{1,0:T(1,128)}) custom-call(bf16[32,8192]{1,0:T(8,128)(2,1)} %get-tuple-element.6.sums_in, f32[1,96]{1,0:T(1,128)} %get-tuple-element.7.norm_in), custom_call_target="tpu_custom_call" | custom-call | tf_op jit(solution)/shard_map/pallas_call | solution.py:765

commit v6 on v5

--- a/solution.py
+++ b/solution.py
@@ -342,6 +342,8 @@
         for g, h in late_pieces:
             hand_over(far_inner, g, h)
         other_image(1)
+        own_far(1).start()
+        other_far(1).start()
         for g, h in late_pieces[:-2]:
             hand_over(far_end, g, h)
 
@@ -424,6 +426,43 @@
         both = PR.at[src, pl.ds(0, 2), :, pl.ds(start * tile, (CUTS[-2 + n] - start) * tile)]
         arrived(both, c_rcv.at[src, n])
 
+    def score_source(i, carry):
+        src = jnp.where(i == 0, b, jnp.where(i == 1, buddy, jnp.where(i == 2, far_inner, far_end)))
+
+        @pl.when(i < 2)
+        def _():
+            from_core(src, 0, 0)
+            from_core(src, 1, len(CUTS) - 1)
+
+        @pl.when((i < 2) | is_inner)
+        def _():
+            S[src] = scores_of(X, src, range(T))
+
+        @pl.when((i >= 2) & is_end)
+        def _():
+            @pl.when(i == 3)
+            def _():
+                hand_over(src, *late_pieces[-2])
+
+            from_core(src, 0, 1)
+            S[src] = scores_of(X, src, range(LOW, CUTS[-2]))
+
+            @pl.when(i == 3)
+            def _():
+                hand_over(src, *late_pieces[-1])
+
+            from_core(src, 1, len(CUTS) - 1)
+            S[src] = S[src] + scores_of(X, src, range(CUTS[-2], T))
+
+        @pl.when(i % 2 == 1)
+        def _():
+            q = i // 2
+            SC[q] = packed(side + q * (1 - 2 * side), 1 - x)
+            score_copy(q).start()
+
+        return carry
+
+    lax.fori_loop(0, 2, score_source, 0)
     @pl.when(is_inner)
     def _():
         arrived(XF.at[c, :, :, pl.ds(*far_strips[0])], xf_rcv.at[0])
@@ -439,48 +478,10 @@
 
         lax.fori_loop(0, 2, far_source, 0)
 
-    def score_source(i, carry):
-        src = jnp.where(i == 0, b, jnp.where(i == 1, buddy, jnp.where(i == 2, far_inner, far_end)))
-
-        @pl.when(i < 2)
-        def _():
-            from_core(src, 0, 0)
-            from_core(src, 1, len(CUTS) - 1)
-
-        @pl.when((i < 2) | is_inner)
-        def _():
-            S[src] = scores_of(X, src, range(T))
-
-        @pl.when((i >= 2) & is_end)
-        def _():
-            @pl.when(i == 3)
-            def _():
-                hand_over(src, *late_pieces[-2])
-
-            from_core(src, 0, 1)
-            S[src] = scores_of(X, src, range(LOW, CUTS[-2]))
-
-            @pl.when(i == 3)
-            def _():
-                hand_over(src, *late_pieces[-1])
-
-            from_core(src, 1, len(CUTS) - 1)
-            S[src] = S[src] + scores_of(X, src, range(CUTS[-2], T))
-
-        @pl.when(i % 2 == 1)
-        def _():
-            q = i // 2
-            SC[q] = packed(side + q * (1 - 2 * side), 1 - x)
-            score_copy(q).start()
-
-        return carry
-
-    lax.fori_loop(0, 4, score_source, 0)
+    lax.fori_loop(2, 4, score_source, 0)
 
     @pl.when(is_end)
     def _():
-        own_far(1).start()
-        other_far(1).start()
         arrived(FR, f_rcv.at[0])
         for k, src in enumerate((far_inner, far_end)):
             S[src, x] = S[src, x] + FR[k, 0] + FR[k, 1]
@@ -567,12 +568,19 @@
 
     @pl.when(is_end)
     def _():
-        def send(t, carry):
-            for k, q, d in ((1, 0, far_end), (0, 0, far_inner), (2, 1, inner)):
-                if k != 0:
-                    multiply(q, t, False)
-                TE[k, t - TF] = own(t, q, d).astype(jnp.bfloat16)
-                end_copy(k, t - TF).start()
+        def send(k, q, d, t):
+            TE[k, t - TF] = own(t, q, d).astype(jnp.bfloat16)
+            end_copy(k, t - TF).start()
+
+        def send_far(t, carry):
+            multiply(0, t, False)
+            send(1, 0, far_end, t)
+            send(0, 0, far_inner, t)
+            return carry
+
+        def send_near(t, carry):
+            multiply(1, t, False)
+            send(2, 1, inner, t)
             return carry
 
         def pass_on(t, carry):
@@ -589,7 +597,8 @@
             return carry
 
         left(QP, qf_snd.at[0])
-        lax.fori_loop(TF, T, send, 0)
+        lax.fori_loop(TF, T, send_far, 0)
+        lax.fori_loop(TF, T, send_near, 0)
         lax.fori_loop(0, TF, pass_on, 0)
         lax.fori_loop(TF, T, finish, 0)
 
@@ -634,9 +643,9 @@
                 multiply_any(0, t)
                 outward(1, far_end, t)
 
-            @pl.when((t >= 2) & (t < T + 2))
-            def _():
-                outward(0, far_inner, t - 2)
+            @pl.when((t >= 3) & (t < T + 3))
+            def _():
+                outward(0, far_inner, t - 3)
 
             @pl.when(t == 1)
             def _():
@@ -653,9 +662,9 @@
                 TI[n] = (own(n, 1, end) + f32(RM[1, n])).astype(jnp.bfloat16)
                 inner_copy(n).start()
 
-            @pl.when(t >= 4)
-            def _():
-                n = t - 4
+            @pl.when(t >= 5)
+            def _():
+                n = t - 5
                 arrived(RM.at[0, n], m_rcv.at[0, n])
                 total = own(n, 1, inner) + f32(RM[0, n])
 
@@ -673,7 +682,7 @@
 
             return carry
 
-        lax.fori_loop(0, T + 4, turn, 0)
+        lax.fori_loop(0, T + 5, turn, 0)
 
     left(QP.at[0], q_snd.at[0])
     left(QP.at[0, 0], q_snd.at[1])

time: 76.8 us -> 75.5 us (0.983)
  Pallas kernels: 76.1 us -> 74.7 us
    pallas_call x1, Pallas kernels: 74.1 us -> 72.7 us  [paired_halves(): pl.pallas_call(paired, out_shape=(jax.ShapeDtypeStruct((refs, coef), bf16...]
where the time goes in v6:
time: 75.5 us; the launch traced here: 75.3 us
  Pallas kernels  74.7 us (99%)
    pallas_call x1, Pallas kernels, paired_halves(): pl.pallas_call(paired, out_shape=(jax.ShapeDtypeStruct((refs, coef), bf16...  72.7 us
    pallas_call x1, Pallas kernels, paired_halves(): pl.pallas_call(hand_out, grid=(coef // block,), out_shape=(jax.ShapeDtype...  1.97 us

profile of v6, /device:TPU:0, one launch (start us, length us, event | category | flops | bytes accessed | tf_op | source)
XLA Modules:
  0.0 75.3 jit_solution(3188235526869666492)
XLA Ops:
  0.6 72.7 %shard_map.59 = (bf16[32,8192]{1,0:T(8,128)(2,1)}, f32[1,96]{1,0:T(1,128)}) custom-call(bf16[96,8192]{1,0:T(8,128)(2,1)} %images.1, s32[2,96]{1,0:T(2,128)} %bitcast.6, bf16[32,8192]{1,0:T(8,128)(2,1)} %bitcast.5, f32[8192]{0:T(1024)} %noise_in.1), custom_call_target="tpu_custom_call" | custom-call | flops 1610612736 | bytes 3145728 | tf_op jit(solution)/shard_map/pallas_call | solution.py:723
  73.3 2.0 %shard_map.60 = (f32[32,8192]{1,0:T(8,128)}, f32[1,96]{1,0:T(1,128)}) custom-call(bf16[32,8192]{1,0:T(8,128)(2,1)} %get-tuple-element.6.sums_in, f32[1,96]{1,0:T(1,128)} %get-tuple-element.7.norm_in), custom_call_target="tpu_custom_call" | custom-call | tf_op jit(solution)/shard_map/pallas_call | solution.py:774

commit v7 on v6

--- a/solution.py
+++ b/solution.py
@@ -341,8 +341,8 @@
         other_far(0).start()
         for g, h in late_pieces:
             hand_over(far_inner, g, h)
+        own_far(1).start()
         other_image(1)
-        own_far(1).start()
         other_far(1).start()
         for g, h in late_pieces[:-2]:
             hand_over(far_end, g, h)
@@ -504,7 +504,7 @@
         value = jnp.exp(chunks[q] - normalizer)
         QP[p, c, x] = for_core(value, c)
         QO[p] = for_core(value, 1 - c)
-        for k in (0, 2, 1):
+        for k in (2, 0, 1):
             post_copy(k, p).start()
 
         @pl.when(is_end)

time: 75.5 us -> 74.8 us (level)
  no operation moved by 1% of the time
where the time goes in v7:
time: 74.8 us; the launch traced here: 74.7 us
  Pallas kernels  74 us (99%)
    pallas_call x1, Pallas kernels, paired_halves(): pl.pallas_call(paired, out_shape=(jax.ShapeDtypeStruct((refs, coef), bf16...  72 us
    pallas_call x1, Pallas kernels, paired_halves(): pl.pallas_call(hand_out, grid=(coef // block,), out_shape=(jax.ShapeDtype...  1.97 us

profile of v7, /device:TPU:0, one launch (start us, length us, event | category | flops | bytes accessed | tf_op | source)
XLA Modules:
  0.0 74.7 jit_solution(9938827646618451493)
XLA Ops:
  0.6 72.0 %shard_map.59 = (bf16[32,8192]{1,0:T(8,128)(2,1)}, f32[1,96]{1,0:T(1,128)}) custom-call(bf16[96,8192]{1,0:T(8,128)(2,1)} %images.1, s32[2,96]{1,0:T(2,128)} %bitcast.6, bf16[32,8192]{1,0:T(8,128)(2,1)} %bitcast.5, f32[8192]{0:T(1024)} %noise_in.1), custom_call_target="tpu_custom_call" | custom-call | flops 1610612736 | bytes 3145728 | tf_op jit(solution)/shard_map/pallas_call | solution.py:723
  72.7 2.0 %shard_map.60 = (f32[32,8192]{1,0:T(8,128)}, f32[1,96]{1,0:T(1,128)}) custom-call(bf16[32,8192]{1,0:T(8,128)(2,1)} %get-tuple-element.6.sums_in, f32[1,96]{1,0:T(1,128)} %get-tuple-element.7.norm_in), custom_call_target="tpu_custom_call" | custom-call | tf_op jit(solution)/shard_map/pallas_call | solution.py:774

commit v8 on v7

--- a/solution.py
+++ b/solution.py
@@ -637,15 +637,17 @@
 
             middle_copy(k, t).start()
 
+        lead = 4
+
         def turn(t, carry):
             @pl.when(t < T)
             def _():
                 multiply_any(0, t)
                 outward(1, far_end, t)
 
-            @pl.when((t >= 3) & (t < T + 3))
-            def _():
-                outward(0, far_inner, t - 3)
+            @pl.when((t >= lead) & (t < T + lead))
+            def _():
+                outward(0, far_inner, t - lead)
 
             @pl.when(t == 1)
             def _():
@@ -662,9 +664,9 @@
                 TI[n] = (own(n, 1, end) + f32(RM[1, n])).astype(jnp.bfloat16)
                 inner_copy(n).start()
 
-            @pl.when(t >= 5)
-            def _():
-                n = t - 5
+            @pl.when(t >= 8)
+            def _():
+                n = t - 8
                 arrived(RM.at[0, n], m_rcv.at[0, n])
                 total = own(n, 1, inner) + f32(RM[0, n])
 
@@ -682,7 +684,7 @@
 
             return carry
 
-        lax.fori_loop(0, T + 5, turn, 0)
+        lax.fori_loop(0, T + 8, turn, 0)
 
     left(QP.at[0], q_snd.at[0])
     left(QP.at[0, 0], q_snd.at[1])

time: 74.8 us -> 73.5 us (0.983)
  Pallas kernels: 74 us -> 72.6 us
    pallas_call x1, Pallas kernels: 72 us -> 70.6 us  [paired_halves(): pl.pallas_call(paired, out_shape=(jax.ShapeDtypeStruct((refs, coef), bf16...]
where the time goes in v8:
time: 73.5 us; the launch traced here: 73.2 us
  Pallas kernels  72.6 us (99%)
    pallas_call x1, Pallas kernels, paired_halves(): pl.pallas_call(paired, out_shape=(jax.ShapeDtypeStruct((refs, coef), bf16...  70.6 us
    pallas_call x1, Pallas kernels, paired_halves(): pl.pallas_call(hand_out, grid=(coef // block,), out_shape=(jax.ShapeDtype...  1.97 us

profile of v8, /device:TPU:0, one launch (start us, length us, event | category | flops | bytes accessed | tf_op | source)
XLA Modules:
  0.0 73.2 jit_solution(17891189541166130270)
XLA Ops:
  0.6 70.6 %shard_map.59 = (bf16[32,8192]{1,0:T(8,128)(2,1)}, f32[1,96]{1,0:T(1,128)}) custom-call(bf16[96,8192]{1,0:T(8,128)(2,1)} %images.1, s32[2,96]{1,0:T(2,128)} %bitcast.6, bf16[32,8192]{1,0:T(8,128)(2,1)} %bitcast.5, f32[8192]{0:T(1024)} %noise_in.1), custom_call_target="tpu_custom_call" | custom-call | flops 1610612736 | bytes 3145728 | tf_op jit(solution)/shard_map/pallas_call | solution.py:725
  71.3 2.0 %shard_map.60 = (f32[32,8192]{1,0:T(8,128)}, f32[1,96]{1,0:T(1,128)}) custom-call(bf16[32,8192]{1,0:T(8,128)(2,1)} %get-tuple-element.6.sums_in, f32[1,96]{1,0:T(1,128)} %get-tuple-element.7.norm_in), custom_call_target="tpu_custom_call" | custom-call | tf_op jit(solution)/shard_map/pallas_call | solution.py:776
